TPU v7x, 256 devices: a whole 4x4x8 slice. The times are simulated.
256 devices in a mesh: segment: 4 (over y), dp: 64 (over x, z, core).
Axes of the slice: x: 4, y: 4, z: 8, core: 2. Of those that a mesh axis runs over, the one named last changes fastest.
Arguments:
- images: bfloat16 [2, 512, 32, 768], P(None, 'dp'), may hold values from -6 to 6
- dw_weight: bfloat16 [4, 7, 7, 768], P('segment'), may hold values from -0.875 to 0.875
- dw_bias: float32 [4, 768], P('segment'), may hold values from -3 to 3
- ln_gain: float32 [4, 768], P('segment'), may hold values from 0.5 to 2
- ln_bias: float32 [4, 768], P('segment'), may hold values from -3 to 3
- w_in: bfloat16 [4, 768, 3072], P('segment'), may hold values from -0.21875 to 0.21875
- b_in: float32 [4, 3072], P('segment'), may hold values from -3 to 3
- w_out: bfloat16 [4, 3072, 768], P('segment'), may hold values from -0.109375 to 0.109375
- b_out: float32 [4, 768], P('segment'), may hold values from -3 to 3
- layer_scale: float32 [4, 768], P('segment'), may hold values from 0.25 to 1
Outputs:
- stash: bfloat16 [4, 2, 512, 32, 768], P('segment', None, 'dp')
All inputs are finite; a program needn't handle non-finite values.
Results may differ from a plain program's by a relative error of at most 0.015.
Values may be sent and summed in bfloat16 or wider, within the bound.
No kernel may reach another device: no remote copies, remote signals or barrier semaphores. Data moves between devices by JAX's collectives and lax.ppermute only.
A program may use at most 128 MiB of HBM per device.

v0:
```python
import functools

import jax
import jax.numpy as jnp
import numpy as np
from jax import lax
from jax.experimental import pallas as pl
from jax.experimental.pallas import tpu as pltpu
from jax.sharding import PartitionSpec as P

SIDE = 32
TAPS = 7
REACH = 3
CROSS = 3
NEAR = 3
LANES = 128
SUBLANES = 16
BF = jnp.bfloat16
F32 = jnp.float32
VECTORS = 5


def own_row(flip, rows, row):
    return flip * (rows - 1) + (1 - 2 * flip) * row


def run_copies(copies, sems):
    copies = [pltpu.make_async_copy(a, b, sems.at[i]) for i, (a, b) in enumerate(copies)]
    for copy in copies:
        copy.start()
    return copies


def rows_kernel(flags, images, *rest):
    micros, rows = images.shape[:2]
    sems = rest[-1]
    copies = []
    for m in range(micros):
        near, far, cross = rest[m], rest[micros + m], rest[2 * micros]
        for row in range(rows):
            here = images.at[m, own_row(flags[1], rows, row)]
            copies.append((here, near.at[row] if row < NEAR else far.at[row - NEAR]))
            if row >= rows - CROSS:
                copies.append((here, cross.at[m, row - (rows - CROSS)]))
    for copy in run_copies(copies, sems):
        copy.wait()


def mirrored_rows(flags, images):
    micros, rows, width, channels = images.shape
    return pl.pallas_call(
        rows_kernel,
        out_shape=[pltpu.VMEM((NEAR, width, channels), BF)] * micros
        + [pltpu.VMEM((rows - NEAR, width, channels), BF)] * micros
        + [pltpu.VMEM((micros, CROSS, width, channels), BF)],
        in_specs=[pl.BlockSpec(memory_space=pltpu.SMEM), pl.BlockSpec(memory_space=pltpu.HBM)],
        out_specs=[pl.BlockSpec(memory_space=pltpu.VMEM)] * (2 * micros + 1),
        scratch_shapes=[pltpu.SemaphoreType.DMA((micros * (rows + CROSS),))],
        compiler_params=pltpu.CompilerParams(vmem_limit_bytes=2**20),
        cost_estimate=pl.CostEstimate(flops=0, bytes_accessed=2 * rows * width * channels, transcendentals=0),
        name="mirrored_rows",
    )(flags, pltpu.with_memory_space_constraint(images, pltpu.HBM))


def setup_kernel(flags, weight, conv_bias, gain, shift, b_out, scale, b_in, taps, vectors, inner, select, raw, sems):
    copies = [(v, vectors.at[i]) for i, v in enumerate((conv_bias, gain, shift, b_out, scale))]
    copies += [(b_in, inner)]
    copies += [(weight.at[0, jnp.where(flags[1] == 1, TAPS - 1 - i, i)], raw.at[i]) for i in range(TAPS)]
    copies = run_copies(copies, sems)
    width, depth = select.shape
    at = lax.broadcasted_iota(jnp.int32, (width, depth), 0)
    entry = lax.broadcasted_iota(jnp.int32, (width, depth), 1)
    hit = jnp.zeros((width, depth), jnp.bool_)
    for col in range(TAPS):
        hit = hit | ((entry - col * width == at + col - REACH) & (entry >= col * width) & (entry < (col + 1) * width))
    select[...] = hit.astype(F32).astype(BF)
    for copy in copies:
        copy.wait()
    for off in range(TAPS):
        rows = raw[off].astype(F32)
        for col in range(TAPS):
            one = jnp.broadcast_to(rows[col : col + 1, :], (SUBLANES, rows.shape[1]))
            taps[off * TAPS + col] = one.astype(BF)


def setup(flags, weight, vectors, b_in, width):
    channels = weight.shape[-1]
    operands = [pltpu.with_memory_space_constraint(v, pltpu.HBM) for v in (weight, *vectors, b_in)]
    return pl.pallas_call(
        setup_kernel,
        out_shape=[
            pltpu.VMEM((TAPS * TAPS, SUBLANES, channels), BF),
            pltpu.VMEM((VECTORS, 1, channels), F32),
            pltpu.VMEM(b_in.shape, F32),
            pltpu.VMEM((width, TAPS * width), BF),
        ],
        in_specs=[pl.BlockSpec(memory_space=pltpu.SMEM)] + [pl.BlockSpec(memory_space=pltpu.HBM)] * len(operands),
        out_specs=[pl.BlockSpec(memory_space=pltpu.VMEM)] * 4,
        scratch_shapes=[
            pltpu.VMEM((TAPS, TAPS, channels), BF),
            pltpu.SemaphoreType.DMA((VECTORS + 1 + TAPS,)),
        ],
        compiler_params=pltpu.CompilerParams(vmem_limit_bytes=4 * 2**20),
        cost_estimate=pl.CostEstimate(flops=0, bytes_accessed=2**22, transcendentals=0),
        name="setup",
    )(flags, *operands)


def block_kernel(micro, last, final, chunk, *refs):
    refs = list(refs)
    flags, near, far, swap, cross, taps, vectors, inner_bias, select, w_in_hbm, w_out_hbm = refs[:11]
    w_in, w_out, sums, normal, total, *tail = refs[-7 if last else -6 :]
    sems = tail[-1]
    outs = refs[11 : -7 if last else -6]
    if last:
        earlier, stash, result = outs[0], outs[-1], tail[0]
    else:
        result = outs[-1]
    near_out, far_out, cross_out = (None, None, None) if final else outs[-4:-1]
    rows, width, channels = near.shape[0] + far.shape[0], near.shape[1], near.shape[2]
    cross = cross.at[micro] if len(cross.shape) == 4 else cross
    hidden = w_in.shape[1]
    conv_bias, gain, shift, b_out, scale = (vectors.at[i] for i in range(VECTORS))

    def source(row, lanes):
        if row < REACH:
            return swap[REACH - 1 - row, :, lanes]
        if row < REACH + NEAR:
            return near[row - REACH, :, lanes]
        if row < REACH + rows:
            return far[row - REACH - NEAR, :, lanes]
        return cross[REACH + CROSS + rows - 1 - row, :, lanes]

    @pl.when(flags[0] == 1)
    def _():
        get_in = pltpu.make_async_copy(w_in_hbm, w_in, sems.at[0])
        get_out = pltpu.make_async_copy(w_out_hbm, w_out, sems.at[1])
        get_in.start()
        get_out.start()
        if last:
            keep_earlier = pltpu.make_async_copy(earlier, stash.at[0, micro - 1], sems.at[2])
            keep_earlier.start()
        @pl.loop(0, channels // LANES)
        def _(group):
            lanes = pl.ds(pl.multiple_of(group * LANES, LANES), LANES)
            inputs = [source(row, lanes) for row in range(rows + 2 * REACH)]
            for col in range(TAPS):
                parts = [None] * rows
                for off in range(TAPS):
                    tap = taps[off * TAPS + col, :, lanes]
                    tap = jnp.concatenate([tap] * (width // SUBLANES), axis=0)
                    for row in range(rows):
                        term = inputs[row + off] * tap
                        parts[row] = term if off == 0 else parts[row] + term
                for row in range(rows):
                    sums[row, col * width : (col + 1) * width, lanes] = parts[row]

        @pl.loop(0, rows, unroll=2)
        def _(row):
            conv = jnp.dot(select[...], sums[row], preferred_element_type=F32) + conv_bias[...]
            centred = conv - jnp.mean(conv, axis=-1, keepdims=True)
            var = jnp.mean(centred * centred, axis=-1, keepdims=True)
            normed = (centred * lax.rsqrt(var + 1e-06) * gain[...] + shift[...]).astype(BF)
            normal[pl.ds(pl.multiple_of(row * width, width), width), :] = normed

        get_in.wait()
        for start in range(0, hidden, chunk):
            part = slice(start, start + chunk)
            inner = jnp.dot(normal[...], w_in[:, part], preferred_element_type=F32) + inner_bias[:, part]
            act = (0.5 * inner * (1.0 + lax.erf(inner * np.float32(0.5**0.5)))).astype(BF)
            if start == 0:
                get_out.wait()
            branch = jnp.dot(act, w_out[part, :], preferred_element_type=F32)
            if start == 0:
                total[...] = branch
            else:
                total[...] += branch
        def outcome(row, value):
            branch = total[pl.ds(pl.multiple_of(row * width, width), width), :] + b_out[...]
            value = (value.astype(F32) + scale[...] * branch).astype(BF)
            result[own_row(flags[1], rows, row)] = value
            return value

        @pl.loop(0, NEAR)
        def _(row):
            value = outcome(row, near[row])
            if not final:
                near_out[row] = value

        @pl.loop(0, rows - NEAR)
        def _(row):
            value = outcome(row + NEAR, far[row])
            if not final:
                far_out[row] = value
                if rows - NEAR == CROSS:
                    cross_out[row] = value
                else:

                    @pl.when(row >= rows - NEAR - CROSS)
                    def _():
                        cross_out[jnp.maximum(row - (rows - NEAR - CROSS), 0)] = value

        if last:
            keep = pltpu.make_async_copy(result, stash.at[0, micro], sems.at[3])
            keep.start()
            keep_earlier.wait()
            keep.wait()


def run_block(micro, micros, final, flags, halo, params, weights, earlier, stash):
    last = micro == micros - 1
    near, far = halo[:2]
    rows, width, channels = near.shape[0] + far.shape[0], near.shape[1], near.shape[2]
    vmem = pl.BlockSpec(memory_space=pltpu.VMEM)
    anywhere = pl.BlockSpec(memory_space=pl.ANY)
    held = [pltpu.with_memory_space_constraint(v, pltpu.VMEM) for v in [*halo, *params]]
    pinned = [pltpu.with_memory_space_constraint(v, pltpu.HBM) for v in weights]
    operands = [flags] + held + pinned
    specs = [pl.BlockSpec(memory_space=pltpu.SMEM)] + [vmem] * len(held)
    specs += [pl.BlockSpec(memory_space=pltpu.HBM)] * len(pinned)
    counts = () if final else (NEAR, rows - NEAR, CROSS)
    out_shape = [pltpu.VMEM((count, width, channels), BF) for count in counts]
    scratch = [
        pltpu.VMEM(weights[0].shape, BF),
        pltpu.VMEM(weights[1].shape, BF),
        pltpu.VMEM((rows, TAPS * width, channels), BF),
        pltpu.VMEM((rows * width, channels), BF),
        pltpu.VMEM((rows * width, channels), F32),
    ]
    result = pltpu.VMEM((rows, width, channels), BF)
    out_specs = [vmem] * len(out_shape)
    aliases = {}
    if last:
        operands.append(pltpu.with_memory_space_constraint(earlier, pltpu.VMEM))
        specs.append(vmem)
        if stash is not None:
            aliases = {len(operands): len(out_shape)}
            operands.append(stash)
            specs.append(anywhere)
        out_shape.append(jax.ShapeDtypeStruct((1, micros, rows, width, channels), BF))
        out_specs.append(anywhere)
        scratch.append(result)
    else:
        out_shape.append(result)
        out_specs.append(vmem)
    *relayed, kept = pl.pallas_call(
        functools.partial(block_kernel, micro, last, final, 768),
        out_shape=out_shape,
        in_specs=specs,
        out_specs=out_specs,
        scratch_shapes=scratch + [pltpu.SemaphoreType.DMA((4,))],
        input_output_aliases=aliases,
        compiler_params=pltpu.CompilerParams(vmem_limit_bytes=32 * 2**20),
        cost_estimate=pl.CostEstimate(flops=2**33 if last else 2**33, bytes_accessed=2**10, transcendentals=0),
        name="block",
    )(*operands)
    return relayed, kept


def body(images, dw_weight, dw_bias, ln_gain, ln_bias, w_in, b_in, w_out, b_out, layer_scale):
    segment = lax.axis_index("segment")
    sections = lax.axis_size("segment")
    place = lax.axis_index("dp")
    places = lax.axis_size("dp")
    micros, rows, width, channels = images.shape
    per_image = SIDE // rows
    half = per_image // 2
    reverse = (place % 2 == 0).astype(jnp.int32)
    flags = [jnp.stack([(segment == section).astype(jnp.int32), reverse]) for section in range(sections)]

    axes = ("segment", "dp")

    def index(section, p):
        return section % sections * places + p % places

    facing = {}
    for p in range(places):
        if (p + half) % per_image in (half - 1, half):
            facing[p] = p + 1 if p % 2 == 1 else p - 1
    swap_pairs = [(index(s, p), index(s, p ^ 1)) for s in range(sections) for p in range(places)]
    near_pairs = [(index(s, p), index(s, q)) for s in range(sections) for p, q in facing.items()]

    def relay_pairs(section, onward):
        return [(index(section, p), index(section + 1, q)) for p, q in onward.items()]

    same = {p: p for p in range(places)}

    *parts, cross = mirrored_rows(flags[0], images)
    cross = lax.ppermute(cross, axes, near_pairs)
    params = setup(flags[0], dw_weight, (dw_bias, ln_gain, ln_bias, b_out, layer_scale), b_in, width)
    weights = (w_in[0], w_out[0])

    halos = [(parts[m], parts[micros + m], cross) for m in range(micros)]
    stash = before = None
    for section in range(sections):
        later, earlier = [], None
        for m in range(micros):
            near, far, cross = halos[m]
            if section > 0:
                near, _ = lax.optimization_barrier((near, before))
            swap = lax.ppermute(near, axes, swap_pairs)
            halo = (near, far, swap, cross)
            final = section == sections - 1
            relayed, kept = run_block(m, micros, final, flags[section], halo, params, weights, earlier, stash)
            before = kept
            if m == micros - 1:
                stash = kept
            else:
                earlier = kept
            if not final:
                near = lax.ppermute(relayed[0], axes, relay_pairs(section, same))
                cross = lax.ppermute(relayed[2], axes, relay_pairs(section, facing))
                far = lax.ppermute(relayed[1], axes, relay_pairs(section, same))
                later.append((near, far, cross))
        halos = later
    return stash


def solution(mesh):
    in_specs = (
        P(None, "dp", None, None),
        P("segment", None, None, None),
        P("segment", None),
        P("segment", None),
        P("segment", None),
        P("segment", None, None),
        P("segment", None),
        P("segment", None, None),
        P("segment", None),
        P("segment", None),
    )
    out_specs = P("segment", None, "dp", None, None)
    return jax.shard_map(body, mesh=mesh, in_specs=in_specs, out_specs=out_specs, check_vma=False)
```

profile of v0, /device:TPU:24, one launch (start us, length us, event | category | flops | bytes accessed | tf_op | source)
XLA Modules:
  0.0 103.0 jit_solution(11100554304935190311)
XLA Ops:
  0.1 1.9 %mirrored_rows.1 = (bf16[3,32,768]{2,1,0:T(8,128)(2,1)S(1)}, bf16[3,32,768]{2,1,0:T(8,128)(2,1)S(1)}, bf16[5,32,768]{2,1,0:T(8,128)(2,1)S(1)}, bf16[5,32,768]{2,...) custom-call(s32[2]{0:T(128)S(1)} %pad_add_fusion.3.flags.refs_0_, bf16[2,8,32,768]{3,2,1,0:T(8,128)(2,1)} %images.1), custom_call_target="tpu_custom_call" | custom-call | bytes 393216 | tf_op jit(solution)/shard_map/mirrored_rows/pallas_call | solution.py:51
  2.0 9.4 %collective-permute-start.1 = (bf16[2,3,32,768]{3,2,1,0:T(8,128)(2,1)S(1)}, bf16[2,3,32,768]{3,2,1,0:T(8,128)(2,1)S(1)}, u32[]{:S(2)}, u32[]{:S(2)}) collective-permute-start(bf16[2,3,32,768]{3,2,1,0:T(8,128)(2,1)S(1)} %get-tuple-element.46), channel_id=1, source_target_pairs={{0,63},{3,4},{4,3},{7,8},{8,7},{11,12},{12,11},{15,16},{16,15},{19... | collective-permute-start | bytes 884744 | tf_op jit(solution)/shard_map/ppermute | solution.py:289
  12.0 1.6 %setup.1 = (bf16[49,16,768]{2,1,0:T(8,128)(2,1)S(1)}, f32[5,1,768]{2,1,0:T(1,128)S(1)}, f32[1,3072]{1,0:T(1,128)S(1)}, bf16[32,224]{1,0:T(8,128)(2,1)S(1)}) custom-call(s32[2]{0:T(128)S(1)} %pad_add_fusion.3.flags.refs_0_, bf16[1,7,7,768]{3,2,1,0:T(8,128)(2,1)} %weight.1, f32[1,768]{1,0:T(1,128)} %conv_bias.1, f32[1,768]{1,0:T(1,128)} %gain.1, ...), custom_call_target="tpu_custom_call" | custom-call | bytes 4194304 | tf_op jit(solution)/shard_map/setup/pallas_call | solution.py:89
  13.7 2.2 %collective-permute-done.1.refs_4_ = bf16[2,3,32,768]{3,2,1,0:T(8,128)(2,1)S(1)} collective-permute-done((bf16[2,3,32,768]{3,2,1,0:T(8,128)(2,1)S(1)}, bf16[2,3,32,768]{3,2,1,0:T(8,128)(2,1)S(1)}, u32[]{:S(2)}, u32[]{:S(2)}) %collective-permute-start.1) | collective-permute-done | bytes 294944 | tf_op jit(solution)/shard_map/ppermute | solution.py:289
  16.4 0.7 collective-permute-start.4
  17.1 0.7 collective-permute-start.7
  17.8 0.7 collective-permute-start.5
  19.9 0.7 collective-permute-start.10
  20.6 0.7 collective-permute-start.8
  21.9 0.8 collective-permute-start.9
  24.0 0.7 collective-permute-start.13
  26.9 0.7 collective-permute-start.16
  28.8 1.3 %collective-permute-start.20 = (bf16[3,32,768]{2,1,0:T(8,128)(2,1)S(1)}, bf16[3,32,768]{2,1,0:T(8,128)(2,1)S(1)}, u32[]{:S(2)}, u32[]{:S(2)}) collective-permute-start(bf16[3,32,768]{2,1,0:T(8,128)(2,1)S(1)} %get-tuple-element.75), channel_id=1, source_target_pairs={{128,192},{129,193},{130,194},{131,195},{132,196},{133,197},{134,1... | collective-permute-start | bytes 442376 | tf_op jit(solution)/shard_map/ppermute | solution.py:311
  30.1 1.3 %collective-permute-start.23 = (bf16[3,32,768]{2,1,0:T(8,128)(2,1)S(1)}, bf16[3,32,768]{2,1,0:T(8,128)(2,1)S(1)}, u32[]{:S(2)}, u32[]{:S(2)}) collective-permute-start(bf16[3,32,768]{2,1,0:T(8,128)(2,1)S(1)} %get-tuple-element.79), channel_id=1, source_target_pairs={{128,255},{131,196},{132,195},{135,200},{136,199},{139,204},{140,2... | collective-permute-start | bytes 442376 | tf_op jit(solution)/shard_map/ppermute | solution.py:312
  31.4 1.3 %collective-permute-start.21 = (bf16[5,32,768]{2,1,0:T(8,128)(2,1)S(1)}, bf16[5,32,768]{2,1,0:T(8,128)(2,1)S(1)}, u32[]{:S(2)}, u32[]{:S(2)}) collective-permute-start(bf16[5,32,768]{2,1,0:T(8,128)(2,1)S(1)} %get-tuple-element.78), channel_id=1, source_target_pairs={{128,192},{129,193},{130,194},{131,195},{132,196},{133,197},{134,1... | collective-permute-start | bytes 737288 | tf_op jit(solution)/shard_map/ppermute | solution.py:313
  33.3 38.5 %collective-permute-done.20.refs_1_ = bf16[3,32,768]{2,1,0:T(8,128)(2,1)S(1)} collective-permute-done((bf16[3,32,768]{2,1,0:T(8,128)(2,1)S(1)}, bf16[3,32,768]{2,1,0:T(8,128)(2,1)S(1)}, u32[]{:S(2)}, u32[]{:S(2)}) %collective-permute-start.20) | collective-permute-done | bytes 147488 | tf_op jit(solution)/shard_map/ppermute | solution.py:311
  71.9 1.3 %collective-permute-start.19 = (bf16[3,32,768]{2,1,0:T(8,128)(2,1)S(1)}, bf16[3,32,768]{2,1,0:T(8,128)(2,1)S(1)}, u32[]{:S(2)}, u32[]{:S(2)}) collective-permute-start(bf16[3,32,768]{2,1,0:T(8,128)(2,1)S(1)} %get-tuple-element.74), channel_id=1, source_target_pairs={{128,192},{129,193},{130,194},{131,195},{132,196},{133,197},{134,1... | collective-permute-start | bytes 442376 | tf_op jit(solution)/shard_map/ppermute | solution.py:311
  73.2 1.3 %collective-permute-start.26 = (bf16[3,32,768]{2,1,0:T(8,128)(2,1)S(1)}, bf16[3,32,768]{2,1,0:T(8,128)(2,1)S(1)}, u32[]{:S(2)}, u32[]{:S(2)}) collective-permute-start(bf16[3,32,768]{2,1,0:T(8,128)(2,1)S(1)} %get-tuple-element.82), channel_id=1, source_target_pairs={{128,255},{131,196},{132,195},{135,200},{136,199},{139,204},{140,2... | collective-permute-start | bytes 442376 | tf_op jit(solution)/shard_map/ppermute | solution.py:312
  74.5 3.0 %collective-permute-done.23.refs_4_ = bf16[3,32,768]{2,1,0:T(8,128)(2,1)S(1)} collective-permute-done((bf16[3,32,768]{2,1,0:T(8,128)(2,1)S(1)}, bf16[3,32,768]{2,1,0:T(8,128)(2,1)S(1)}, u32[]{:S(2)}, u32[]{:S(2)}) %collective-permute-start.23) | collective-permute-done | bytes 147488 | tf_op jit(solution)/shard_map/ppermute | solution.py:312
  77.5 1.3 %collective-permute-start.24 = (bf16[5,32,768]{2,1,0:T(8,128)(2,1)S(1)}, bf16[5,32,768]{2,1,0:T(8,128)(2,1)S(1)}, u32[]{:S(2)}, u32[]{:S(2)}) collective-permute-start(bf16[5,32,768]{2,1,0:T(8,128)(2,1)S(1)} %get-tuple-element.81), channel_id=1, source_target_pairs={{128,192},{129,193},{130,194},{131,195},{132,196},{133,197},{134,1... | collective-permute-start | bytes 737288 | tf_op jit(solution)/shard_map/ppermute | solution.py:313
  78.8 8.2 %block.14.refs_11_ = bf16[8,32,768]{2,1,0:T(8,128)(2,1)S(1)} custom-call(s32[2]{0:T(128)S(1)} %pad_add_fusion.refs_0_, bf16[3,32,768]{2,1,0:T(8,128)(2,1)S(1)} %collective-permute-done.20.refs_1_, bf16[5,32,768]{2,1,0:T(8,128)(2,1)S(1)} %collective-permute-done.21.refs_2_, bf16[3,32,768]{2,1,0:T(8,128)(2,1)S(1)} %collective-permute-done.22.refs_3_, ...), custom_call_target="tpu_custom_call" | custom-call | flops 8589934592 | bytes 1024 | tf_op jit(solution)/shard_map/block/pallas_call | solution.py:246
  87.4 4.0 %collective-permute-done.26.refs_4_ = bf16[3,32,768]{2,1,0:T(8,128)(2,1)S(1)} collective-permute-done((bf16[3,32,768]{2,1,0:T(8,128)(2,1)S(1)}, bf16[3,32,768]{2,1,0:T(8,128)(2,1)S(1)}, u32[]{:S(2)}, u32[]{:S(2)}) %collective-permute-start.26) | collective-permute-done | bytes 147488 | tf_op jit(solution)/shard_map/ppermute | solution.py:312
  91.5 2.6 %collective-permute-done.24.refs_2_ = bf16[5,32,768]{2,1,0:T(8,128)(2,1)S(1)} collective-permute-done((bf16[5,32,768]{2,1,0:T(8,128)(2,1)S(1)}, bf16[5,32,768]{2,1,0:T(8,128)(2,1)S(1)}, u32[]{:S(2)}, u32[]{:S(2)}) %collective-permute-start.24) | collective-permute-done | bytes 245792 | tf_op jit(solution)/shard_map/ppermute | solution.py:313
  94.1 8.7 %block.15 = bf16[1,2,8,32,768]{4,3,2,1,0:T(8,128)(2,1)} custom-call(s32[2]{0:T(128)S(1)} %pad_add_fusion.refs_0_, bf16[3,32,768]{2,1,0:T(8,128)(2,1)S(1)} %collective-permute-done.19.refs_1_, bf16[5,32,768]{2,1,0:T(8,128)(2,1)S(1)} %collective-permute-done.24.refs_2_, ...), custom_call_target="tpu_custom_call", output_to_operand_aliasing={{}: (12, {})} | custom-call | flops 8589934592 | bytes 1024 | tf_op jit(solution)/shard_map/block/pallas_call | solution.py:246
  (44 shorter events, 9.0 us)
Async XLA Ops:
  2.0 13.8 %collective-permute-start.1 = (bf16[2,3,32,768]{3,2,1,0:T(8,128)(2,1)S(1)}, bf16[2,3,32,768]{3,2,1,0:T(8,128)(2,1)S(1)}, u32[]{:S(2)}, u32[]{:S(2)}) collective-permute-start(bf16[2,3,32,768]{3,2,1,0:T(8,128)(2,1)S(1)} %get-tuple-element.46), channel_id=1, source_target_pairs={{0,63},{3,4},{4,3},{7,8},{8,7},{11,12},{12,11},{15,16},{16,15},{19... | collective-permute-start | bytes 884744 | tf_op jit(solution)/shard_map/ppermute | solution.py:289
  11.5 6.9 %collective-permute-start = (bf16[3,32,768]{2,1,0:T(8,128)(2,1)S(1)}, bf16[3,32,768]{2,1,0:T(8,128)(2,1)S(1)}, u32[]{:S(2)}, u32[]{:S(2)}) collective-permute-start(bf16[3,32,768]{2,1,0:T(8,128)(2,1)S(1)} %get-tuple-element.44.refs_1_), channel_id=1, source_target_pairs={{0,1},{1,0},{2,3},{3,2},{4,5},{5,4},{6,7},{7,6},{8,9},{9,8},{10,11... | collective-permute-start | bytes 442376 | tf_op jit(solution)/shard_map/ppermute | solution.py:301
  16.4 2.6 %collective-permute-start.4 = (bf16[3,32,768]{2,1,0:T(8,128)(2,1)S(1)}, bf16[3,32,768]{2,1,0:T(8,128)(2,1)S(1)}, u32[]{:S(2)}, u32[]{:S(2)}) collective-permute-start(bf16[3,32,768]{2,1,0:T(8,128)(2,1)S(1)} %get-tuple-element.55), channel_id=1, source_target_pairs={{0,64},{1,65},{2,66},{3,67},{4,68},{5,69},{6,70},{7,71},{8,72},{9,... | collective-permute-start | bytes 442376 | tf_op jit(solution)/shard_map/ppermute | solution.py:311
  17.1 3.5 %collective-permute-start.7 = (bf16[3,32,768]{2,1,0:T(8,128)(2,1)S(1)}, bf16[3,32,768]{2,1,0:T(8,128)(2,1)S(1)}, u32[]{:S(2)}, u32[]{:S(2)}) collective-permute-start(bf16[3,32,768]{2,1,0:T(8,128)(2,1)S(1)} %get-tuple-element.59), channel_id=1, source_target_pairs={{0,127},{3,68},{4,67},{7,72},{8,71},{11,76},{12,75},{15,80},{16,79... | collective-permute-start | bytes 442376 | tf_op jit(solution)/shard_map/ppermute | solution.py:312
  17.8 3.5 %collective-permute-start.5 = (bf16[5,32,768]{2,1,0:T(8,128)(2,1)S(1)}, bf16[5,32,768]{2,1,0:T(8,128)(2,1)S(1)}, u32[]{:S(2)}, u32[]{:S(2)}) collective-permute-start(bf16[5,32,768]{2,1,0:T(8,128)(2,1)S(1)} %get-tuple-element.58), channel_id=1, source_target_pairs={{0,64},{1,65},{2,66},{3,67},{4,68},{5,69},{6,70},{7,71},{8,72},{9,... | collective-permute-start | bytes 737288 | tf_op jit(solution)/shard_map/ppermute | solution.py:313
  19.3 2.7 %collective-permute-start.3 = (bf16[3,32,768]{2,1,0:T(8,128)(2,1)S(1)}, bf16[3,32,768]{2,1,0:T(8,128)(2,1)S(1)}, u32[]{:S(2)}, u32[]{:S(2)}) collective-permute-start(bf16[3,32,768]{2,1,0:T(8,128)(2,1)S(1)} %get-tuple-element.54), channel_id=1, source_target_pairs={{0,64},{1,65},{2,66},{3,67},{4,68},{5,69},{6,70},{7,71},{8,72},{9,... | collective-permute-start | bytes 442376 | tf_op jit(solution)/shard_map/ppermute | solution.py:311
  19.9 4.1 %collective-permute-start.10 = (bf16[3,32,768]{2,1,0:T(8,128)(2,1)S(1)}, bf16[3,32,768]{2,1,0:T(8,128)(2,1)S(1)}, u32[]{:S(2)}, u32[]{:S(2)}) collective-permute-start(bf16[3,32,768]{2,1,0:T(8,128)(2,1)S(1)} %get-tuple-element.63), channel_id=1, source_target_pairs={{0,127},{3,68},{4,67},{7,72},{8,71},{11,76},{12,75},{15,80},{16,79... | collective-permute-start | bytes 442376 | tf_op jit(solution)/shard_map/ppermute | solution.py:312
  20.6 4.1 %collective-permute-start.8 = (bf16[5,32,768]{2,1,0:T(8,128)(2,1)S(1)}, bf16[5,32,768]{2,1,0:T(8,128)(2,1)S(1)}, u32[]{:S(2)}, u32[]{:S(2)}) collective-permute-start(bf16[5,32,768]{2,1,0:T(8,128)(2,1)S(1)} %get-tuple-element.62), channel_id=1, source_target_pairs={{0,64},{1,65},{2,66},{3,67},{4,68},{5,69},{6,70},{7,71},{8,72},{9,... | collective-permute-start | bytes 737288 | tf_op jit(solution)/shard_map/ppermute | solution.py:313
  21.9 2.8 %collective-permute-start.9 = (bf16[3,32,768]{2,1,0:T(8,128)(2,1)S(1)}, bf16[3,32,768]{2,1,0:T(8,128)(2,1)S(1)}, u32[]{:S(2)}, u32[]{:S(2)}) collective-permute-start(bf16[3,32,768]{2,1,0:T(8,128)(2,1)S(1)} %collective-permute-done.3.refs_1_), channel_id=1, source_target_pairs={{0,1},{1,0},{2,3},{3,2},{4,5},{5,4},{6,7},{7,6},{8,9},{9,8},{10,11... | collective-permute-start | bytes 442376 | tf_op jit(solution)/shard_map/ppermute | solution.py:301
  22.7 2.7 %collective-permute-start.12 = (bf16[3,32,768]{2,1,0:T(8,128)(2,1)S(1)}, bf16[3,32,768]{2,1,0:T(8,128)(2,1)S(1)}, u32[]{:S(2)}, u32[]{:S(2)}) collective-permute-start(bf16[3,32,768]{2,1,0:T(8,128)(2,1)S(1)} %get-tuple-element.65), channel_id=1, source_target_pairs={{64,128},{65,129},{66,130},{67,131},{68,132},{69,133},{70,134},{71... | collective-permute-start | bytes 442376 | tf_op jit(solution)/shard_map/ppermute | solution.py:311
  23.4 3.5 %collective-permute-start.15 = (bf16[3,32,768]{2,1,0:T(8,128)(2,1)S(1)}, bf16[3,32,768]{2,1,0:T(8,128)(2,1)S(1)}, u32[]{:S(2)}, u32[]{:S(2)}) collective-permute-start(bf16[3,32,768]{2,1,0:T(8,128)(2,1)S(1)} %get-tuple-element.69), channel_id=1, source_target_pairs={{64,191},{67,132},{68,131},{71,136},{72,135},{75,140},{76,139},{79... | collective-permute-start | bytes 442376 | tf_op jit(solution)/shard_map/ppermute | solution.py:312
  24.0 3.5 %collective-permute-start.13 = (bf16[5,32,768]{2,1,0:T(8,128)(2,1)S(1)}, bf16[5,32,768]{2,1,0:T(8,128)(2,1)S(1)}, u32[]{:S(2)}, u32[]{:S(2)}) collective-permute-start(bf16[5,32,768]{2,1,0:T(8,128)(2,1)S(1)} %get-tuple-element.68), channel_id=1, source_target_pairs={{64,128},{65,129},{66,130},{67,131},{68,132},{69,133},{70,134},{71... | collective-permute-start | bytes 737288 | tf_op jit(solution)/shard_map/ppermute | solution.py:313
  25.5 2.7 %collective-permute-start.11 = (bf16[3,32,768]{2,1,0:T(8,128)(2,1)S(1)}, bf16[3,32,768]{2,1,0:T(8,128)(2,1)S(1)}, u32[]{:S(2)}, u32[]{:S(2)}) collective-permute-start(bf16[3,32,768]{2,1,0:T(8,128)(2,1)S(1)} %get-tuple-element.64), channel_id=1, source_target_pairs={{64,128},{65,129},{66,130},{67,131},{68,132},{69,133},{70,134},{71... | collective-permute-start | bytes 442376 | tf_op jit(solution)/shard_map/ppermute | solution.py:311
  26.2 5.2 %collective-permute-start.18 = (bf16[3,32,768]{2,1,0:T(8,128)(2,1)S(1)}, bf16[3,32,768]{2,1,0:T(8,128)(2,1)S(1)}, u32[]{:S(2)}, u32[]{:S(2)}) collective-permute-start(bf16[3,32,768]{2,1,0:T(8,128)(2,1)S(1)} %get-tuple-element.73), channel_id=1, source_target_pairs={{64,191},{67,132},{68,131},{71,136},{72,135},{75,140},{76,139},{79... | collective-permute-start | bytes 442376 | tf_op jit(solution)/shard_map/ppermute | solution.py:312
  26.9 5.8 %collective-permute-start.16 = (bf16[5,32,768]{2,1,0:T(8,128)(2,1)S(1)}, bf16[5,32,768]{2,1,0:T(8,128)(2,1)S(1)}, u32[]{:S(2)}, u32[]{:S(2)}) collective-permute-start(bf16[5,32,768]{2,1,0:T(8,128)(2,1)S(1)} %get-tuple-element.72), channel_id=1, source_target_pairs={{64,128},{65,129},{66,130},{67,131},{68,132},{69,133},{70,134},{71... | collective-permute-start | bytes 737288 | tf_op jit(solution)/shard_map/ppermute | solution.py:313
  28.2 4.5 %collective-permute-start.17 = (bf16[3,32,768]{2,1,0:T(8,128)(2,1)S(1)}, bf16[3,32,768]{2,1,0:T(8,128)(2,1)S(1)}, u32[]{:S(2)}, u32[]{:S(2)}) collective-permute-start(bf16[3,32,768]{2,1,0:T(8,128)(2,1)S(1)} %collective-permute-done.11.refs_1_), channel_id=1, source_target_pairs={{0,1},{1,0},{2,3},{3,2},{4,5},{5,4},{6,7},{7,6},{8,9},{9,8},{10,11... | collective-permute-start | bytes 442376 | tf_op jit(solution)/shard_map/ppermute | solution.py:301
  28.8 43.1 %collective-permute-start.20 = (bf16[3,32,768]{2,1,0:T(8,128)(2,1)S(1)}, bf16[3,32,768]{2,1,0:T(8,128)(2,1)S(1)}, u32[]{:S(2)}, u32[]{:S(2)}) collective-permute-start(bf16[3,32,768]{2,1,0:T(8,128)(2,1)S(1)} %get-tuple-element.75), channel_id=1, source_target_pairs={{128,192},{129,193},{130,194},{131,195},{132,196},{133,197},{134,1... | collective-permute-start | bytes 442376 | tf_op jit(solution)/shard_map/ppermute | solution.py:311
  30.1 47.4 %collective-permute-start.23 = (bf16[3,32,768]{2,1,0:T(8,128)(2,1)S(1)}, bf16[3,32,768]{2,1,0:T(8,128)(2,1)S(1)}, u32[]{:S(2)}, u32[]{:S(2)}) collective-permute-start(bf16[3,32,768]{2,1,0:T(8,128)(2,1)S(1)} %get-tuple-element.79), channel_id=1, source_target_pairs={{128,255},{131,196},{132,195},{135,200},{136,199},{139,204},{140,2... | collective-permute-start | bytes 442376 | tf_op jit(solution)/shard_map/ppermute | solution.py:312
  31.4 47.4 %collective-permute-start.21 = (bf16[5,32,768]{2,1,0:T(8,128)(2,1)S(1)}, bf16[5,32,768]{2,1,0:T(8,128)(2,1)S(1)}, u32[]{:S(2)}, u32[]{:S(2)}) collective-permute-start(bf16[5,32,768]{2,1,0:T(8,128)(2,1)S(1)} %get-tuple-element.78), channel_id=1, source_target_pairs={{128,192},{129,193},{130,194},{131,195},{132,196},{133,197},{134,1... | collective-permute-start | bytes 737288 | tf_op jit(solution)/shard_map/ppermute | solution.py:313
  71.9 6.9 %collective-permute-start.22 = (bf16[3,32,768]{2,1,0:T(8,128)(2,1)S(1)}, bf16[3,32,768]{2,1,0:T(8,128)(2,1)S(1)}, u32[]{:S(2)}, u32[]{:S(2)}) collective-permute-start(bf16[3,32,768]{2,1,0:T(8,128)(2,1)S(1)} %collective-permute-done.20.refs_1_), channel_id=1, source_target_pairs={{0,1},{1,0},{2,3},{3,2},{4,5},{5,4},{6,7},{7,6},{8,9},{9,8},{10,11... | collective-permute-start | bytes 442376 | tf_op jit(solution)/shard_map/ppermute | solution.py:301
  71.9 15.5 %collective-permute-start.19 = (bf16[3,32,768]{2,1,0:T(8,128)(2,1)S(1)}, bf16[3,32,768]{2,1,0:T(8,128)(2,1)S(1)}, u32[]{:S(2)}, u32[]{:S(2)}) collective-permute-start(bf16[3,32,768]{2,1,0:T(8,128)(2,1)S(1)} %get-tuple-element.74), channel_id=1, source_target_pairs={{128,192},{129,193},{130,194},{131,195},{132,196},{133,197},{134,1... | collective-permute-start | bytes 442376 | tf_op jit(solution)/shard_map/ppermute | solution.py:311
  73.2 18.3 %collective-permute-start.26 = (bf16[3,32,768]{2,1,0:T(8,128)(2,1)S(1)}, bf16[3,32,768]{2,1,0:T(8,128)(2,1)S(1)}, u32[]{:S(2)}, u32[]{:S(2)}) collective-permute-start(bf16[3,32,768]{2,1,0:T(8,128)(2,1)S(1)} %get-tuple-element.82), channel_id=1, source_target_pairs={{128,255},{131,196},{132,195},{135,200},{136,199},{139,204},{140,2... | collective-permute-start | bytes 442376 | tf_op jit(solution)/shard_map/ppermute | solution.py:312
  77.5 16.6 %collective-permute-start.24 = (bf16[5,32,768]{2,1,0:T(8,128)(2,1)S(1)}, bf16[5,32,768]{2,1,0:T(8,128)(2,1)S(1)}, u32[]{:S(2)}, u32[]{:S(2)}) collective-permute-start(bf16[5,32,768]{2,1,0:T(8,128)(2,1)S(1)} %get-tuple-element.81), channel_id=1, source_target_pairs={{128,192},{129,193},{130,194},{131,195},{132,196},{133,197},{134,1... | collective-permute-start | bytes 737288 | tf_op jit(solution)/shard_map/ppermute | solution.py:313
  87.4 6.7 %collective-permute-start.25 = (bf16[3,32,768]{2,1,0:T(8,128)(2,1)S(1)}, bf16[3,32,768]{2,1,0:T(8,128)(2,1)S(1)}, u32[]{:S(2)}, u32[]{:S(2)}) collective-permute-start(bf16[3,32,768]{2,1,0:T(8,128)(2,1)S(1)} %collective-permute-done.19.refs_1_), channel_id=1, source_target_pairs={{0,1},{1,0},{2,3},{3,2},{4,5},{5,4},{6,7},{7,6},{8,9},{9,8},{10,11... | collective-permute-start | bytes 442376 | tf_op jit(solution)/shard_map/ppermute | solution.py:301
  (3 other events, 6.7 us)
where the time goes:
time: 104 us; the launch traced here: 103 us
  waiting for transfers between devices  50.8 us (49%)
  starting transfers between devices  27.3 us (26%)
  Pallas kernels  24 us (23%)
    ppermute x6, waiting for transfers between devices, body(): near = lax.ppermute(relayed[0], axes, relay_pairs(section, same))  39 us
    pallas_call x8, Pallas kernels, run_block(): pl.pallas_call(functools.partial(block_kernel, micro, last, final, 768),...  20.4 us
    ppermute x1, starting transfers between devices, body(): cross = lax.ppermute(cross, axes, near_pairs)  9.4 us
    ppermute x6, waiting for transfers between devices, body(): cross = lax.ppermute(relayed[2], axes, relay_pairs(section, facing))  7 us
    ppermute x6, starting transfers between devices, body(): far = lax.ppermute(relayed[1], axes, relay_pairs(section, same))  5.28 us
    ppermute x6, starting transfers between devices, body(): cross = lax.ppermute(relayed[2], axes, relay_pairs(section, facing))  5.26 us
    ppermute x6, starting transfers between devices, body(): near = lax.ppermute(relayed[0], axes, relay_pairs(section, same))  5.21 us
    ppermute x6, waiting for transfers between devices, body(): far = lax.ppermute(relayed[1], axes, relay_pairs(section, same))  2.63 us
  transfers between devices with their start and end apart: 27, of which 6 were waited for; matrix products, arithmetic and copies ran while one was open for 0% of the time, Pallas kernels for 13%

commit v1 on v0

--- a/solution.py
+++ b/solution.py
@@ -36,10 +36,15 @@
     sems = rest[-1]
     copies = []
     for m in range(micros):
-        near, far, cross = rest[m], rest[micros + m], rest[2 * micros]
+        near, far, cross = rest[2 * m], rest[2 * m + 1], rest[2 * micros]
         for row in range(rows):
             here = images.at[m, own_row(flags[1], rows, row)]
-            copies.append((here, near.at[row] if row < NEAR else far.at[row - NEAR]))
+            if m == micros - 1:
+                copies.append((here, far.at[row]))
+                if row < NEAR:
+                    copies.append((here, near.at[row]))
+            else:
+                copies.append((here, near.at[row] if row < NEAR else far.at[row - NEAR]))
             if row >= rows - CROSS:
                 copies.append((here, cross.at[m, row - (rows - CROSS)]))
     for copy in run_copies(copies, sems):
@@ -48,14 +53,14 @@
 
 def mirrored_rows(flags, images):
     micros, rows, width, channels = images.shape
+    counts = [NEAR, rows - NEAR] * (micros - 1) + [NEAR, rows]
     return pl.pallas_call(
         rows_kernel,
-        out_shape=[pltpu.VMEM((NEAR, width, channels), BF)] * micros
-        + [pltpu.VMEM((rows - NEAR, width, channels), BF)] * micros
+        out_shape=[pltpu.VMEM((count, width, channels), BF) for count in counts]
         + [pltpu.VMEM((micros, CROSS, width, channels), BF)],
         in_specs=[pl.BlockSpec(memory_space=pltpu.SMEM), pl.BlockSpec(memory_space=pltpu.HBM)],
         out_specs=[pl.BlockSpec(memory_space=pltpu.VMEM)] * (2 * micros + 1),
-        scratch_shapes=[pltpu.SemaphoreType.DMA((micros * (rows + CROSS),))],
+        scratch_shapes=[pltpu.SemaphoreType.DMA((micros * (rows + CROSS) + NEAR,))],
         compiler_params=pltpu.CompilerParams(vmem_limit_bytes=2**20),
         cost_estimate=pl.CostEstimate(flops=0, bytes_accessed=2 * rows * width * channels, transcendentals=0),
         name="mirrored_rows",
@@ -108,16 +113,25 @@
 
 def block_kernel(micro, last, final, chunk, *refs):
     refs = list(refs)
-    flags, near, far, swap, cross, taps, vectors, inner_bias, select, w_in_hbm, w_out_hbm = refs[:11]
+    if last:
+        whole = refs.pop(1)
+        rows, width, channels = whole.shape
+        near, far = whole.at[:NEAR], whole.at[NEAR:]
+    else:
+        near, far = refs.pop(1), refs.pop(1)
+        rows, width, channels = near.shape[0] + far.shape[0], near.shape[1], near.shape[2]
+    flags, swap, cross, taps, vectors, inner_bias, select, w_in_hbm, w_out_hbm = refs[:9]
     w_in, w_out, sums, normal, total, *tail = refs[-7 if last else -6 :]
     sems = tail[-1]
-    outs = refs[11 : -7 if last else -6]
+    outs = refs[9 : -7 if last else -6]
     if last:
         earlier, stash, result = outs[0], outs[-1], tail[0]
     else:
         result = outs[-1]
     near_out, far_out, cross_out = (None, None, None) if final else outs[-4:-1]
-    rows, width, channels = near.shape[0] + far.shape[0], near.shape[1], near.shape[2]
+    if last and not final:
+        whole_out = far_out
+        far_out = whole_out.at[NEAR:]
     cross = cross.at[micro] if len(cross.shape) == 4 else cross
     hidden = w_in.shape[1]
     conv_bias, gain, shift, b_out, scale = (vectors.at[i] for i in range(VECTORS))
@@ -186,6 +200,8 @@
             value = outcome(row, near[row])
             if not final:
                 near_out[row] = value
+                if last:
+                    whole_out[row] = value
 
         @pl.loop(0, rows - NEAR)
         def _(row):
@@ -209,8 +225,8 @@
 
 def run_block(micro, micros, final, flags, halo, params, weights, earlier, stash):
     last = micro == micros - 1
-    near, far = halo[:2]
-    rows, width, channels = near.shape[0] + far.shape[0], near.shape[1], near.shape[2]
+    own = halo[:1] if last else halo[:2]
+    rows, (width, channels) = sum(v.shape[0] for v in own), own[0].shape[1:]
     vmem = pl.BlockSpec(memory_space=pltpu.VMEM)
     anywhere = pl.BlockSpec(memory_space=pl.ANY)
     held = [pltpu.with_memory_space_constraint(v, pltpu.VMEM) for v in [*halo, *params]]
@@ -218,7 +234,7 @@
     operands = [flags] + held + pinned
     specs = [pl.BlockSpec(memory_space=pltpu.SMEM)] + [vmem] * len(held)
     specs += [pl.BlockSpec(memory_space=pltpu.HBM)] * len(pinned)
-    counts = () if final else (NEAR, rows - NEAR, CROSS)
+    counts = () if final else (NEAR, rows if last else rows - NEAR, CROSS)
     out_shape = [pltpu.VMEM((count, width, channels), BF) for count in counts]
     scratch = [
         pltpu.VMEM(weights[0].shape, BF),
@@ -251,7 +267,7 @@
         scratch_shapes=scratch + [pltpu.SemaphoreType.DMA((4,))],
         input_output_aliases=aliases,
         compiler_params=pltpu.CompilerParams(vmem_limit_bytes=32 * 2**20),
-        cost_estimate=pl.CostEstimate(flops=2**33 if last else 2**33, bytes_accessed=2**10, transcendentals=0),
+        cost_estimate=pl.CostEstimate(flops=2**20 if last else 2**33, bytes_accessed=2**10, transcendentals=0),
         name="block",
     )(*operands)
     return relayed, kept
@@ -284,22 +300,30 @@
         return [(index(section, p), index(section + 1, q)) for p, q in onward.items()]
 
     same = {p: p for p in range(places)}
+    other = {p: p ^ 1 for p in range(places)}
 
     *parts, cross = mirrored_rows(flags[0], images)
     cross = lax.ppermute(cross, axes, near_pairs)
     params = setup(flags[0], dw_weight, (dw_bias, ln_gain, ln_bias, b_out, layer_scale), b_in, width)
     weights = (w_in[0], w_out[0])
 
-    halos = [(parts[m], parts[micros + m], cross) for m in range(micros)]
+    halos = []
+    for m in range(micros):
+        near, far = parts[2 * m : 2 * m + 2]
+        if m == micros - 1:
+            halos.append((far, lax.ppermute(near, axes, swap_pairs), cross))
+        else:
+            halos.append((near, far, None, cross))
     stash = before = None
     for section in range(sections):
         later, earlier = [], None
         for m in range(micros):
-            near, far, cross = halos[m]
-            if section > 0:
-                near, _ = lax.optimization_barrier((near, before))
-            swap = lax.ppermute(near, axes, swap_pairs)
-            halo = (near, far, swap, cross)
+            halo = halos[m]
+            if m < micros - 1:
+                near, far, _, cross = halo
+                if section > 0:
+                    near, _ = lax.optimization_barrier((near, before))
+                halo = (near, far, lax.ppermute(near, axes, swap_pairs), cross)
             final = section == sections - 1
             relayed, kept = run_block(m, micros, final, flags[section], halo, params, weights, earlier, stash)
             before = kept
@@ -308,10 +332,16 @@
             else:
                 earlier = kept
             if not final:
-                near = lax.ppermute(relayed[0], axes, relay_pairs(section, same))
-                cross = lax.ppermute(relayed[2], axes, relay_pairs(section, facing))
-                far = lax.ppermute(relayed[1], axes, relay_pairs(section, same))
-                later.append((near, far, cross))
+                if m < micros - 1:
+                    near = lax.ppermute(relayed[0], axes, relay_pairs(section, same))
+                    cross = lax.ppermute(relayed[2], axes, relay_pairs(section, facing))
+                    far = lax.ppermute(relayed[1], axes, relay_pairs(section, same))
+                    later.append((near, far, None, cross))
+                else:
+                    near = lax.ppermute(relayed[0], axes, relay_pairs(section, other))
+                    cross = lax.ppermute(relayed[2], axes, relay_pairs(section, facing))
+                    whole = lax.ppermute(relayed[1], axes, relay_pairs(section, same))
+                    later.append((whole, near, cross))
         halos = later
     return stash
 

time: 104 us -> 113 us (1.087)
  waiting for transfers between devices: 50.8 us -> 61.1 us
    ppermute x8 -> x11, waiting for transfers between devices: 0.02 us -> 11 us  [the longest x3 5.78 us: body(): whole = lax.ppermute(relayed[1], axes, relay_pairs(section, same))]
    ppermute x8 -> x11, starting transfers between devices: 2.13 us -> 6.51 us  [the longest x3 2.65 us: body(): whole = lax.ppermute(relayed[1], axes, relay_pairs(section, same))]
    ppermute x6, waiting for transfers between devices: 7 us -> 10.7 us  [body(): cross = lax.ppermute(relayed[2], axes, relay_pairs(section, facing))]
    ppermute x6 -> x3, starting transfers between devices: 5.28 us -> 2.64 us  [body(): far = lax.ppermute(relayed[1], axes, relay_pairs(section, same))]
    ppermute x6 -> x3, waiting for transfers between devices: 2.63 us -> 0.01 us  [body(): far = lax.ppermute(relayed[1], axes, relay_pairs(section, same))]
    ppermute x6 -> x3, starting transfers between devices: 5.21 us -> 2.63 us  [body(): near = lax.ppermute(relayed[0], axes, relay_pairs(section, same))]
    ppermute x6 -> x3, waiting for transfers between devices: 39 us -> 37.1 us  [body(): near = lax.ppermute(relayed[0], axes, relay_pairs(section, same))]
  transfers between devices with their start and end apart: 27 -> 24, of which waited for: 6 -> 6; matrix products, arithmetic and copies ran while one was open for 0% -> 0% of each run, Pallas kernels for 13% -> 12%
where the time goes in v1:
time: 113 us
  waiting for transfers between devices  61.1 us (54%)
  starting transfers between devices  26.4 us (23%)
  Pallas kernels  24.2 us (21%)
    ppermute x3, waiting for transfers between devices, body(): near = lax.ppermute(relayed[0], axes, relay_pairs(section, same))  37.1 us
    pallas_call x8, Pallas kernels, run_block(): pl.pallas_call(functools.partial(block_kernel, micro, last, final, 768),...  20.6 us
    ppermute x6, waiting for transfers between devices, body(): cross = lax.ppermute(relayed[2], axes, relay_pairs(section, facing))  10.7 us
    ppermute x1, starting transfers between devices, body(): cross = lax.ppermute(cross, axes, near_pairs)  9.4 us
    ppermute x3, waiting for transfers between devices, body(): whole = lax.ppermute(relayed[1], axes, relay_pairs(section, same))  5.78 us
    ppermute x6, starting transfers between devices, body(): cross = lax.ppermute(relayed[2], axes, relay_pairs(section, facing))  5.26 us
    ppermute x3, waiting for transfers between devices, body(): near = lax.ppermute(relayed[0], axes, relay_pairs(section, other))  5.24 us
    ppermute x3, starting transfers between devices, body(): whole = lax.ppermute(relayed[1], axes, relay_pairs(section, same))  2.65 us
  transfers between devices with their start and end apart: 24, of which 6 were waited for; matrix products, arithmetic and copies ran while one was open for 0% of the time, Pallas kernels for 12%

profile of v1, /device:TPU:24, one launch (start us, length us, event | category | flops | bytes accessed | tf_op | source)
XLA Modules:
  0.0 112.6 jit_solution(12965546532564819189)
XLA Ops:
  0.1 2.0 %mirrored_rows.1 = (bf16[3,32,768]{2,1,0:T(8,128)(2,1)S(1)}, bf16[5,32,768]{2,1,0:T(8,128)(2,1)S(1)}, bf16[3,32,768]{2,1,0:T(8,128)(2,1)S(1)}, bf16[8,32,768]{2,...) custom-call(s32[2]{0:T(128)S(1)} %pad_add_fusion.3.flags.refs_0_, bf16[2,8,32,768]{3,2,1,0:T(8,128)(2,1)} %images.1), custom_call_target="tpu_custom_call" | custom-call | bytes 393216 | tf_op jit(solution)/shard_map/mirrored_rows/pallas_call | solution.py:57
  2.1 9.4 %collective-permute-start.1 = (bf16[2,3,32,768]{3,2,1,0:T(8,128)(2,1)S(1)}, bf16[2,3,32,768]{3,2,1,0:T(8,128)(2,1)S(1)}, u32[]{:S(2)}, u32[]{:S(2)}) collective-permute-start(bf16[2,3,32,768]{3,2,1,0:T(8,128)(2,1)S(1)} %get-tuple-element.43), channel_id=1, source_target_pairs={{0,63},{3,4},{4,3},{7,8},{8,7},{11,12},{12,11},{15,16},{16,15},{19... | collective-permute-start | bytes 884744 | tf_op jit(solution)/shard_map/ppermute | solution.py:306
  12.1 1.6 %setup.1 = (bf16[49,16,768]{2,1,0:T(8,128)(2,1)S(1)}, f32[5,1,768]{2,1,0:T(1,128)S(1)}, f32[1,3072]{1,0:T(1,128)S(1)}, bf16[32,224]{1,0:T(8,128)(2,1)S(1)}) custom-call(s32[2]{0:T(128)S(1)} %pad_add_fusion.3.flags.refs_0_, bf16[1,7,7,768]{3,2,1,0:T(8,128)(2,1)} %weight.1, f32[1,768]{1,0:T(1,128)} %conv_bias.1, f32[1,768]{1,0:T(1,128)} %gain.1, ...), custom_call_target="tpu_custom_call" | custom-call | bytes 4194304 | tf_op jit(solution)/shard_map/setup/pallas_call | solution.py:94
  13.7 2.2 %collective-permute-done.1.refs_4_.refs_3_ = bf16[2,3,32,768]{3,2,1,0:T(8,128)(2,1)S(1)} collective-permute-done((bf16[2,3,32,768]{3,2,1,0:T(8,128)(2,1)S(1)}, bf16[2,3,32,768]{3,2,1,0:T(8,128)(2,1)S(1)}, u32[]{:S(2)}, u32[]{:S(2)}) %collective-permute-start.1) | collective-permute-done | bytes 294944 | tf_op jit(solution)/shard_map/ppermute | solution.py:306
  16.5 0.7 collective-permute-start.6
  17.2 0.7 collective-permute-start.7
  17.9 0.7 collective-permute-start.9
  20.7 0.7 collective-permute-start.3
  22.7 0.7 collective-permute-start.14
  24.1 0.8 block.11
  26.9 0.7 collective-permute-start.10
  28.2 1.3 %collective-permute-start.20 = (bf16[3,32,768]{2,1,0:T(8,128)(2,1)S(1)}, bf16[3,32,768]{2,1,0:T(8,128)(2,1)S(1)}, u32[]{:S(2)}, u32[]{:S(2)}) collective-permute-start(bf16[3,32,768]{2,1,0:T(8,128)(2,1)S(1)} %get-tuple-element.72), channel_id=1, source_target_pairs={{128,192},{129,193},{130,194},{131,195},{132,196},{133,197},{134,1... | collective-permute-start | bytes 442376 | tf_op jit(solution)/shard_map/ppermute | solution.py:336
  29.5 1.3 %collective-permute-start.21 = (bf16[5,32,768]{2,1,0:T(8,128)(2,1)S(1)}, bf16[5,32,768]{2,1,0:T(8,128)(2,1)S(1)}, u32[]{:S(2)}, u32[]{:S(2)}) collective-permute-start(bf16[5,32,768]{2,1,0:T(8,128)(2,1)S(1)} %get-tuple-element.75), channel_id=1, source_target_pairs={{128,192},{129,193},{130,194},{131,195},{132,196},{133,197},{134,1... | collective-permute-start | bytes 737288 | tf_op jit(solution)/shard_map/ppermute | solution.py:338
  30.8 1.3 %collective-permute-start.23 = (bf16[3,32,768]{2,1,0:T(8,128)(2,1)S(1)}, bf16[3,32,768]{2,1,0:T(8,128)(2,1)S(1)}, u32[]{:S(2)}, u32[]{:S(2)}) collective-permute-start(bf16[3,32,768]{2,1,0:T(8,128)(2,1)S(1)} %get-tuple-element.76), channel_id=1, source_target_pairs={{128,255},{131,196},{132,195},{135,200},{136,199},{139,204},{140,2... | collective-permute-start | bytes 442376 | tf_op jit(solution)/shard_map/ppermute | solution.py:337
  32.7 37.1 %collective-permute-done.20.refs_1_ = bf16[3,32,768]{2,1,0:T(8,128)(2,1)S(1)} collective-permute-done((bf16[3,32,768]{2,1,0:T(8,128)(2,1)S(1)}, bf16[3,32,768]{2,1,0:T(8,128)(2,1)S(1)}, u32[]{:S(2)}, u32[]{:S(2)}) %collective-permute-start.20) | collective-permute-done | bytes 147488 | tf_op jit(solution)/shard_map/ppermute | solution.py:336
  69.9 1.3 %collective-permute-start.18 = (bf16[3,32,768]{2,1,0:T(8,128)(2,1)S(1)}, bf16[3,32,768]{2,1,0:T(8,128)(2,1)S(1)}, u32[]{:S(2)}, u32[]{:S(2)}) collective-permute-start(bf16[3,32,768]{2,1,0:T(8,128)(2,1)S(1)} %get-tuple-element.70), channel_id=1, source_target_pairs={{128,193},{129,192},{130,195},{131,194},{132,197},{133,196},{134,1... | collective-permute-start | bytes 442376 | tf_op jit(solution)/shard_map/ppermute | solution.py:341
  71.2 1.3 %collective-permute-start.19 = (bf16[3,32,768]{2,1,0:T(8,128)(2,1)S(1)}, bf16[3,32,768]{2,1,0:T(8,128)(2,1)S(1)}, u32[]{:S(2)}, u32[]{:S(2)}) collective-permute-start(bf16[3,32,768]{2,1,0:T(8,128)(2,1)S(1)} %get-tuple-element.71), channel_id=1, source_target_pairs={{128,255},{131,196},{132,195},{135,200},{136,199},{139,204},{140,2... | collective-permute-start | bytes 442376 | tf_op jit(solution)/shard_map/ppermute | solution.py:342
  72.5 6.3 %collective-permute-done.23.refs_4_ = bf16[3,32,768]{2,1,0:T(8,128)(2,1)S(1)} collective-permute-done((bf16[3,32,768]{2,1,0:T(8,128)(2,1)S(1)}, bf16[3,32,768]{2,1,0:T(8,128)(2,1)S(1)}, u32[]{:S(2)}, u32[]{:S(2)}) %collective-permute-start.23) | collective-permute-done | bytes 147488 | tf_op jit(solution)/shard_map/ppermute | solution.py:337
  78.8 1.3 %collective-permute-start.17 = (bf16[8,32,768]{2,1,0:T(8,128)(2,1)S(1)}, bf16[8,32,768]{2,1,0:T(8,128)(2,1)S(1)}, u32[]{:S(2)}, u32[]{:S(2)}) collective-permute-start(bf16[8,32,768]{2,1,0:T(8,128)(2,1)S(1)} %get-tuple-element.69), channel_id=1, source_target_pairs={{128,192},{129,193},{130,194},{131,195},{132,196},{133,197},{134,1... | collective-permute-start | bytes 1179656 | tf_op jit(solution)/shard_map/ppermute | solution.py:343
  80.1 8.2 %block.14.refs_10_ = bf16[8,32,768]{2,1,0:T(8,128)(2,1)S(1)} custom-call(s32[2]{0:T(128)S(1)} %pad_add_fusion.refs_0_, bf16[3,32,768]{2,1,0:T(8,128)(2,1)S(1)} %collective-permute-done.20.refs_1_, bf16[5,32,768]{2,1,0:T(8,128)(2,1)S(1)} %collective-permute-done.21.refs_2_, bf16[3,32,768]{2,1,0:T(8,128)(2,1)S(1)} %collective-permute-done.22.refs_3_, ...), custom_call_target="tpu_custom_call" | custom-call | flops 8589934592 | bytes 1024 | tf_op jit(solution)/shard_map/block/pallas_call | solution.py:262
  88.3 5.2 %collective-permute-done.18.refs_2_ = bf16[3,32,768]{2,1,0:T(8,128)(2,1)S(1)} collective-permute-done((bf16[3,32,768]{2,1,0:T(8,128)(2,1)S(1)}, bf16[3,32,768]{2,1,0:T(8,128)(2,1)S(1)}, u32[]{:S(2)}, u32[]{:S(2)}) %collective-permute-start.18) | collective-permute-done | bytes 147488 | tf_op jit(solution)/shard_map/ppermute | solution.py:341
  93.5 4.4 %collective-permute-done.19.refs_3_ = bf16[3,32,768]{2,1,0:T(8,128)(2,1)S(1)} collective-permute-done((bf16[3,32,768]{2,1,0:T(8,128)(2,1)S(1)}, bf16[3,32,768]{2,1,0:T(8,128)(2,1)S(1)}, u32[]{:S(2)}, u32[]{:S(2)}) %collective-permute-start.19) | collective-permute-done | bytes 147488 | tf_op jit(solution)/shard_map/ppermute | solution.py:342
  98.0 5.8 %collective-permute-done.17.refs_1_ = bf16[8,32,768]{2,1,0:T(8,128)(2,1)S(1)} collective-permute-done((bf16[8,32,768]{2,1,0:T(8,128)(2,1)S(1)}, bf16[8,32,768]{2,1,0:T(8,128)(2,1)S(1)}, u32[]{:S(2)}, u32[]{:S(2)}) %collective-permute-start.17) | collective-permute-done | bytes 393248 | tf_op jit(solution)/shard_map/ppermute | solution.py:343
  103.8 8.7 %block.15 = bf16[1,2,8,32,768]{4,3,2,1,0:T(8,128)(2,1)} custom-call(s32[2]{0:T(128)S(1)} %pad_add_fusion.refs_0_, bf16[8,32,768]{2,1,0:T(8,128)(2,1)S(1)} %collective-permute-done.17.refs_1_, bf16[3,32,768]{2,1,0:T(8,128)(2,1)S(1)} %collective-permute-done.18.refs_2_, ...), custom_call_target="tpu_custom_call", output_to_operand_aliasing={{}: (11, {})} | custom-call | flops 1048576 | bytes 1024 | tf_op jit(solution)/shard_map/block/pallas_call | solution.py:262
  (38 shorter events, 8.5 us)
Async XLA Ops:
  2.1 13.8 %collective-permute-start.1 = (bf16[2,3,32,768]{3,2,1,0:T(8,128)(2,1)S(1)}, bf16[2,3,32,768]{3,2,1,0:T(8,128)(2,1)S(1)}, u32[]{:S(2)}, u32[]{:S(2)}) collective-permute-start(bf16[2,3,32,768]{3,2,1,0:T(8,128)(2,1)S(1)} %get-tuple-element.43), channel_id=1, source_target_pairs={{0,63},{3,4},{4,3},{7,8},{8,7},{11,12},{12,11},{15,16},{16,15},{19... | collective-permute-start | bytes 884744 | tf_op jit(solution)/shard_map/ppermute | solution.py:306
  11.5 2.2 %collective-permute-start.2 = (bf16[3,32,768]{2,1,0:T(8,128)(2,1)S(1)}, bf16[3,32,768]{2,1,0:T(8,128)(2,1)S(1)}, u32[]{:S(2)}, u32[]{:S(2)}) collective-permute-start(bf16[3,32,768]{2,1,0:T(8,128)(2,1)S(1)} %get-tuple-element.48.refs_1_), channel_id=1, source_target_pairs={{0,1},{1,0},{2,3},{3,2},{4,5},{5,4},{6,7},{7,6},{8,9},{9,8},{10,11... | collective-permute-start | bytes 442376 | tf_op jit(solution)/shard_map/ppermute | solution.py:326
  11.6 6.9 %collective-permute-start = (bf16[3,32,768]{2,1,0:T(8,128)(2,1)S(1)}, bf16[3,32,768]{2,1,0:T(8,128)(2,1)S(1)}, u32[]{:S(2)}, u32[]{:S(2)}) collective-permute-start(bf16[3,32,768]{2,1,0:T(8,128)(2,1)S(1)} %get-tuple-element.42), channel_id=1, source_target_pairs={{0,1},{1,0},{2,3},{3,2},{4,5},{5,4},{6,7},{7,6},{8,9},{9,8},{10,11... | collective-permute-start | bytes 442376 | tf_op jit(solution)/shard_map/ppermute | solution.py:314
  16.5 2.6 %collective-permute-start.6 = (bf16[3,32,768]{2,1,0:T(8,128)(2,1)S(1)}, bf16[3,32,768]{2,1,0:T(8,128)(2,1)S(1)}, u32[]{:S(2)}, u32[]{:S(2)}) collective-permute-start(bf16[3,32,768]{2,1,0:T(8,128)(2,1)S(1)} %get-tuple-element.54), channel_id=1, source_target_pairs={{0,64},{1,65},{2,66},{3,67},{4,68},{5,69},{6,70},{7,71},{8,72},{9,... | collective-permute-start | bytes 442376 | tf_op jit(solution)/shard_map/ppermute | solution.py:336
  17.2 4.2 %collective-permute-start.7 = (bf16[5,32,768]{2,1,0:T(8,128)(2,1)S(1)}, bf16[5,32,768]{2,1,0:T(8,128)(2,1)S(1)}, u32[]{:S(2)}, u32[]{:S(2)}) collective-permute-start(bf16[5,32,768]{2,1,0:T(8,128)(2,1)S(1)} %get-tuple-element.57), channel_id=1, source_target_pairs={{0,64},{1,65},{2,66},{3,67},{4,68},{5,69},{6,70},{7,71},{8,72},{9,... | collective-permute-start | bytes 737288 | tf_op jit(solution)/shard_map/ppermute | solution.py:338
  17.9 2.8 %collective-permute-start.9 = (bf16[3,32,768]{2,1,0:T(8,128)(2,1)S(1)}, bf16[3,32,768]{2,1,0:T(8,128)(2,1)S(1)}, u32[]{:S(2)}, u32[]{:S(2)}) collective-permute-start(bf16[3,32,768]{2,1,0:T(8,128)(2,1)S(1)} %get-tuple-element.58), channel_id=1, source_target_pairs={{0,127},{3,68},{4,67},{7,72},{8,71},{11,76},{12,75},{15,80},{16,79... | collective-permute-start | bytes 442376 | tf_op jit(solution)/shard_map/ppermute | solution.py:337
  19.2 2.2 %collective-permute-start.8 = (bf16[3,32,768]{2,1,0:T(8,128)(2,1)S(1)}, bf16[3,32,768]{2,1,0:T(8,128)(2,1)S(1)}, u32[]{:S(2)}, u32[]{:S(2)}) collective-permute-start(bf16[3,32,768]{2,1,0:T(8,128)(2,1)S(1)} %collective-permute-done.6.refs_1_), channel_id=1, source_target_pairs={{0,1},{1,0},{2,3},{3,2},{4,5},{5,4},{6,7},{7,6},{8,9},{9,8},{10,11... | collective-permute-start | bytes 442376 | tf_op jit(solution)/shard_map/ppermute | solution.py:326
  19.3 4.0 %collective-permute-start.4 = (bf16[3,32,768]{2,1,0:T(8,128)(2,1)S(1)}, bf16[3,32,768]{2,1,0:T(8,128)(2,1)S(1)}, u32[]{:S(2)}, u32[]{:S(2)}) collective-permute-start(bf16[3,32,768]{2,1,0:T(8,128)(2,1)S(1)} %get-tuple-element.52), channel_id=1, source_target_pairs={{0,65},{1,64},{2,67},{3,66},{4,69},{5,68},{6,71},{7,70},{8,73},{9,... | collective-permute-start | bytes 442376 | tf_op jit(solution)/shard_map/ppermute | solution.py:341
  20.0 4.1 %collective-permute-start.5 = (bf16[3,32,768]{2,1,0:T(8,128)(2,1)S(1)}, bf16[3,32,768]{2,1,0:T(8,128)(2,1)S(1)}, u32[]{:S(2)}, u32[]{:S(2)}) collective-permute-start(bf16[3,32,768]{2,1,0:T(8,128)(2,1)S(1)} %get-tuple-element.53), channel_id=1, source_target_pairs={{0,127},{3,68},{4,67},{7,72},{8,71},{11,76},{12,75},{15,80},{16,79... | collective-permute-start | bytes 442376 | tf_op jit(solution)/shard_map/ppermute | solution.py:342
  20.7 3.4 %collective-permute-start.3 = (bf16[8,32,768]{2,1,0:T(8,128)(2,1)S(1)}, bf16[8,32,768]{2,1,0:T(8,128)(2,1)S(1)}, u32[]{:S(2)}, u32[]{:S(2)}) collective-permute-start(bf16[8,32,768]{2,1,0:T(8,128)(2,1)S(1)} %get-tuple-element.51), channel_id=1, source_target_pairs={{0,64},{1,65},{2,66},{3,67},{4,68},{5,69},{6,70},{7,71},{8,72},{9,... | collective-permute-start | bytes 1179656 | tf_op jit(solution)/shard_map/ppermute | solution.py:343
  22.0 2.9 %collective-permute-start.13 = (bf16[3,32,768]{2,1,0:T(8,128)(2,1)S(1)}, bf16[3,32,768]{2,1,0:T(8,128)(2,1)S(1)}, u32[]{:S(2)}, u32[]{:S(2)}) collective-permute-start(bf16[3,32,768]{2,1,0:T(8,128)(2,1)S(1)} %get-tuple-element.63), channel_id=1, source_target_pairs={{64,128},{65,129},{66,130},{67,131},{68,132},{69,133},{70,134},{71... | collective-permute-start | bytes 442376 | tf_op jit(solution)/shard_map/ppermute | solution.py:336
  22.7 4.9 %collective-permute-start.14 = (bf16[5,32,768]{2,1,0:T(8,128)(2,1)S(1)}, bf16[5,32,768]{2,1,0:T(8,128)(2,1)S(1)}, u32[]{:S(2)}, u32[]{:S(2)}) collective-permute-start(bf16[5,32,768]{2,1,0:T(8,128)(2,1)S(1)} %get-tuple-element.66), channel_id=1, source_target_pairs={{64,128},{65,129},{66,130},{67,131},{68,132},{69,133},{70,134},{71... | collective-permute-start | bytes 737288 | tf_op jit(solution)/shard_map/ppermute | solution.py:338
  23.4 3.5 %collective-permute-start.16 = (bf16[3,32,768]{2,1,0:T(8,128)(2,1)S(1)}, bf16[3,32,768]{2,1,0:T(8,128)(2,1)S(1)}, u32[]{:S(2)}, u32[]{:S(2)}) collective-permute-start(bf16[3,32,768]{2,1,0:T(8,128)(2,1)S(1)} %get-tuple-element.67), channel_id=1, source_target_pairs={{64,191},{67,132},{68,131},{71,136},{72,135},{75,140},{76,139},{79... | collective-permute-start | bytes 442376 | tf_op jit(solution)/shard_map/ppermute | solution.py:337
  24.9 2.7 %collective-permute-start.15 = (bf16[3,32,768]{2,1,0:T(8,128)(2,1)S(1)}, bf16[3,32,768]{2,1,0:T(8,128)(2,1)S(1)}, u32[]{:S(2)}, u32[]{:S(2)}) collective-permute-start(bf16[3,32,768]{2,1,0:T(8,128)(2,1)S(1)} %collective-permute-done.13.refs_1_), channel_id=1, source_target_pairs={{0,1},{1,0},{2,3},{3,2},{4,5},{5,4},{6,7},{7,6},{8,9},{9,8},{10,11... | collective-permute-start | bytes 442376 | tf_op jit(solution)/shard_map/ppermute | solution.py:326
  25.5 5.3 %collective-permute-start.11 = (bf16[3,32,768]{2,1,0:T(8,128)(2,1)S(1)}, bf16[3,32,768]{2,1,0:T(8,128)(2,1)S(1)}, u32[]{:S(2)}, u32[]{:S(2)}) collective-permute-start(bf16[3,32,768]{2,1,0:T(8,128)(2,1)S(1)} %get-tuple-element.61), channel_id=1, source_target_pairs={{64,129},{65,128},{66,131},{67,130},{68,133},{69,132},{70,135},{71... | collective-permute-start | bytes 442376 | tf_op jit(solution)/shard_map/ppermute | solution.py:341
  26.2 5.9 %collective-permute-start.12 = (bf16[3,32,768]{2,1,0:T(8,128)(2,1)S(1)}, bf16[3,32,768]{2,1,0:T(8,128)(2,1)S(1)}, u32[]{:S(2)}, u32[]{:S(2)}) collective-permute-start(bf16[3,32,768]{2,1,0:T(8,128)(2,1)S(1)} %get-tuple-element.62), channel_id=1, source_target_pairs={{64,191},{67,132},{68,131},{71,136},{72,135},{75,140},{76,139},{79... | collective-permute-start | bytes 442376 | tf_op jit(solution)/shard_map/ppermute | solution.py:342
  26.9 5.2 %collective-permute-start.10 = (bf16[8,32,768]{2,1,0:T(8,128)(2,1)S(1)}, bf16[8,32,768]{2,1,0:T(8,128)(2,1)S(1)}, u32[]{:S(2)}, u32[]{:S(2)}) collective-permute-start(bf16[8,32,768]{2,1,0:T(8,128)(2,1)S(1)} %get-tuple-element.60), channel_id=1, source_target_pairs={{64,128},{65,129},{66,130},{67,131},{68,132},{69,133},{70,134},{71... | collective-permute-start | bytes 1179656 | tf_op jit(solution)/shard_map/ppermute | solution.py:343
  28.2 41.6 %collective-permute-start.20 = (bf16[3,32,768]{2,1,0:T(8,128)(2,1)S(1)}, bf16[3,32,768]{2,1,0:T(8,128)(2,1)S(1)}, u32[]{:S(2)}, u32[]{:S(2)}) collective-permute-start(bf16[3,32,768]{2,1,0:T(8,128)(2,1)S(1)} %get-tuple-element.72), channel_id=1, source_target_pairs={{128,192},{129,193},{130,194},{131,195},{132,196},{133,197},{134,1... | collective-permute-start | bytes 442376 | tf_op jit(solution)/shard_map/ppermute | solution.py:336
  29.5 50.6 %collective-permute-start.21 = (bf16[5,32,768]{2,1,0:T(8,128)(2,1)S(1)}, bf16[5,32,768]{2,1,0:T(8,128)(2,1)S(1)}, u32[]{:S(2)}, u32[]{:S(2)}) collective-permute-start(bf16[5,32,768]{2,1,0:T(8,128)(2,1)S(1)} %get-tuple-element.75), channel_id=1, source_target_pairs={{128,192},{129,193},{130,194},{131,195},{132,196},{133,197},{134,1... | collective-permute-start | bytes 737288 | tf_op jit(solution)/shard_map/ppermute | solution.py:338
  30.8 48.0 %collective-permute-start.23 = (bf16[3,32,768]{2,1,0:T(8,128)(2,1)S(1)}, bf16[3,32,768]{2,1,0:T(8,128)(2,1)S(1)}, u32[]{:S(2)}, u32[]{:S(2)}) collective-permute-start(bf16[3,32,768]{2,1,0:T(8,128)(2,1)S(1)} %get-tuple-element.76), channel_id=1, source_target_pairs={{128,255},{131,196},{132,195},{135,200},{136,199},{139,204},{140,2... | collective-permute-start | bytes 442376 | tf_op jit(solution)/shard_map/ppermute | solution.py:337
  69.8 10.3 %collective-permute-start.22 = (bf16[3,32,768]{2,1,0:T(8,128)(2,1)S(1)}, bf16[3,32,768]{2,1,0:T(8,128)(2,1)S(1)}, u32[]{:S(2)}, u32[]{:S(2)}) collective-permute-start(bf16[3,32,768]{2,1,0:T(8,128)(2,1)S(1)} %collective-permute-done.20.refs_1_), channel_id=1, source_target_pairs={{0,1},{1,0},{2,3},{3,2},{4,5},{5,4},{6,7},{7,6},{8,9},{9,8},{10,11... | collective-permute-start | bytes 442376 | tf_op jit(solution)/shard_map/ppermute | solution.py:326
  69.9 23.6 %collective-permute-start.18 = (bf16[3,32,768]{2,1,0:T(8,128)(2,1)S(1)}, bf16[3,32,768]{2,1,0:T(8,128)(2,1)S(1)}, u32[]{:S(2)}, u32[]{:S(2)}) collective-permute-start(bf16[3,32,768]{2,1,0:T(8,128)(2,1)S(1)} %get-tuple-element.70), channel_id=1, source_target_pairs={{128,193},{129,192},{130,195},{131,194},{132,197},{133,196},{134,1... | collective-permute-start | bytes 442376 | tf_op jit(solution)/shard_map/ppermute | solution.py:341
  71.2 26.8 %collective-permute-start.19 = (bf16[3,32,768]{2,1,0:T(8,128)(2,1)S(1)}, bf16[3,32,768]{2,1,0:T(8,128)(2,1)S(1)}, u32[]{:S(2)}, u32[]{:S(2)}) collective-permute-start(bf16[3,32,768]{2,1,0:T(8,128)(2,1)S(1)} %get-tuple-element.71), channel_id=1, source_target_pairs={{128,255},{131,196},{132,195},{135,200},{136,199},{139,204},{140,2... | collective-permute-start | bytes 442376 | tf_op jit(solution)/shard_map/ppermute | solution.py:342
  78.8 25.0 %collective-permute-start.17 = (bf16[8,32,768]{2,1,0:T(8,128)(2,1)S(1)}, bf16[8,32,768]{2,1,0:T(8,128)(2,1)S(1)}, u32[]{:S(2)}, u32[]{:S(2)}) collective-permute-start(bf16[8,32,768]{2,1,0:T(8,128)(2,1)S(1)} %get-tuple-element.69), channel_id=1, source_target_pairs={{128,192},{129,193},{130,194},{131,195},{132,196},{133,197},{134,1... | collective-permute-start | bytes 1179656 | tf_op jit(solution)/shard_map/ppermute | solution.py:343

commit v2 on v0

--- a/solution.py
+++ b/solution.py
@@ -155,7 +155,7 @@
                 for row in range(rows):
                     sums[row, col * width : (col + 1) * width, lanes] = parts[row]
 
-        @pl.loop(0, rows, unroll=2)
+        @pl.loop(0, rows, unroll=8)
         def _(row):
             conv = jnp.dot(select[...], sums[row], preferred_element_type=F32) + conv_bias[...]
             centred = conv - jnp.mean(conv, axis=-1, keepdims=True)
@@ -179,15 +179,21 @@
             branch = total[pl.ds(pl.multiple_of(row * width, width), width), :] + b_out[...]
             value = (value.astype(F32) + scale[...] * branch).astype(BF)
             result[own_row(flags[1], rows, row)] = value
+            if last:
+                keep(row).start()
             return value
 
-        @pl.loop(0, NEAR)
+        def keep(row):
+            at = own_row(flags[1], rows, row)
+            return pltpu.make_async_copy(result.at[at], stash.at[0, micro, at], sems.at[3])
+
+        @pl.loop(0, NEAR, unroll=True)
         def _(row):
             value = outcome(row, near[row])
             if not final:
                 near_out[row] = value
 
-        @pl.loop(0, rows - NEAR)
+        @pl.loop(0, rows - NEAR, unroll=True)
         def _(row):
             value = outcome(row + NEAR, far[row])
             if not final:
@@ -201,10 +207,8 @@
                         cross_out[jnp.maximum(row - (rows - NEAR - CROSS), 0)] = value
 
         if last:
-            keep = pltpu.make_async_copy(result, stash.at[0, micro], sems.at[3])
-            keep.start()
             keep_earlier.wait()
-            keep.wait()
+            pltpu.make_async_copy(result, stash.at[0, micro], sems.at[3]).wait()
 
 
 def run_block(micro, micros, final, flags, halo, params, weights, earlier, stash):

time: 104 us -> 98.8 us (0.950)
  waiting for transfers between devices: 50.8 us -> 47.9 us
  Pallas kernels: 24 us -> 22.2 us
    ppermute x6, waiting for transfers between devices: 39 us -> 36.4 us  [body(): near = lax.ppermute(relayed[0], axes, relay_pairs(section, same))]
    pallas_call x8, Pallas kernels: 20.4 us -> 18.6 us  [run_block(): pl.pallas_call(functools.partial(block_kernel, micro, last, final, 768),...]
  transfers between devices with their start and end apart: 27 -> 27, of which waited for: 6 -> 7; matrix products, arithmetic and copies ran while one was open for 0% -> 0% of each run, Pallas kernels for 13% -> 13%
where the time goes in v2:
time: 98.8 us; the launch traced here: 98.3 us
  waiting for transfers between devices  47.9 us (48%)
  starting transfers between devices  27.3 us (28%)
  Pallas kernels  22.2 us (22%)
    ppermute x6, waiting for transfers between devices, body(): near = lax.ppermute(relayed[0], axes, relay_pairs(section, same))  36.4 us
    pallas_call x8, Pallas kernels, run_block(): pl.pallas_call(functools.partial(block_kernel, micro, last, final, 768),...  18.6 us
    ppermute x1, starting transfers between devices, body(): cross = lax.ppermute(cross, axes, near_pairs)  9.4 us
    ppermute x6, waiting for transfers between devices, body(): cross = lax.ppermute(relayed[2], axes, relay_pairs(section, facing))  6.3 us
    ppermute x6, starting transfers between devices, body(): far = lax.ppermute(relayed[1], axes, relay_pairs(section, same))  5.28 us
    ppermute x6, starting transfers between devices, body(): cross = lax.ppermute(relayed[2], axes, relay_pairs(section, facing))  5.26 us
    ppermute x6, starting transfers between devices, body(): near = lax.ppermute(relayed[0], axes, relay_pairs(section, same))  5.21 us
    ppermute x6, waiting for transfers between devices, body(): far = lax.ppermute(relayed[1], axes, relay_pairs(section, same))  3.08 us
  transfers between devices with their start and end apart: 27, of which 7 were waited for; matrix products, arithmetic and copies ran while one was open for 0% of the time, Pallas kernels for 13%

profile of v2, /device:TPU:24, one launch (start us, length us, event | category | flops | bytes accessed | tf_op | source)
XLA Modules:
  0.0 98.3 jit_solution(578323720018692874)
XLA Ops:
  0.1 1.9 %mirrored_rows.1 = (bf16[3,32,768]{2,1,0:T(8,128)(2,1)S(1)}, bf16[3,32,768]{2,1,0:T(8,128)(2,1)S(1)}, bf16[5,32,768]{2,1,0:T(8,128)(2,1)S(1)}, bf16[5,32,768]{2,...) custom-call(s32[2]{0:T(128)S(1)} %pad_add_fusion.3.flags.refs_0_, bf16[2,8,32,768]{3,2,1,0:T(8,128)(2,1)} %images.1), custom_call_target="tpu_custom_call" | custom-call | bytes 393216 | tf_op jit(solution)/shard_map/mirrored_rows/pallas_call | solution.py:51
  2.0 9.4 %collective-permute-start.1 = (bf16[2,3,32,768]{3,2,1,0:T(8,128)(2,1)S(1)}, bf16[2,3,32,768]{3,2,1,0:T(8,128)(2,1)S(1)}, u32[]{:S(2)}, u32[]{:S(2)}) collective-permute-start(bf16[2,3,32,768]{3,2,1,0:T(8,128)(2,1)S(1)} %get-tuple-element.46), channel_id=1, source_target_pairs={{0,63},{3,4},{4,3},{7,8},{8,7},{11,12},{12,11},{15,16},{16,15},{19... | collective-permute-start | bytes 884744 | tf_op jit(solution)/shard_map/ppermute | solution.py:293
  12.0 1.6 %setup.1 = (bf16[49,16,768]{2,1,0:T(8,128)(2,1)S(1)}, f32[5,1,768]{2,1,0:T(1,128)S(1)}, f32[1,3072]{1,0:T(1,128)S(1)}, bf16[32,224]{1,0:T(8,128)(2,1)S(1)}) custom-call(s32[2]{0:T(128)S(1)} %pad_add_fusion.3.flags.refs_0_, bf16[1,7,7,768]{3,2,1,0:T(8,128)(2,1)} %weight.1, f32[1,768]{1,0:T(1,128)} %conv_bias.1, f32[1,768]{1,0:T(1,128)} %gain.1, ...), custom_call_target="tpu_custom_call" | custom-call | bytes 4194304 | tf_op jit(solution)/shard_map/setup/pallas_call | solution.py:89
  13.7 2.2 %collective-permute-done.1.refs_4_ = bf16[2,3,32,768]{3,2,1,0:T(8,128)(2,1)S(1)} collective-permute-done((bf16[2,3,32,768]{3,2,1,0:T(8,128)(2,1)S(1)}, bf16[2,3,32,768]{3,2,1,0:T(8,128)(2,1)S(1)}, u32[]{:S(2)}, u32[]{:S(2)}) %collective-permute-start.1) | collective-permute-done | bytes 294944 | tf_op jit(solution)/shard_map/ppermute | solution.py:293
  16.4 0.7 collective-permute-start.4
  17.8 0.7 collective-permute-start.5
  20.6 0.7 collective-permute-start.8
  21.3 0.8 block.10
  24.0 0.7 collective-permute-start.13
  26.9 0.7 collective-permute-start.16
  28.2 0.8 collective-permute-start.17
  29.0 1.3 %collective-permute-start.20 = (bf16[3,32,768]{2,1,0:T(8,128)(2,1)S(1)}, bf16[3,32,768]{2,1,0:T(8,128)(2,1)S(1)}, u32[]{:S(2)}, u32[]{:S(2)}) collective-permute-start(bf16[3,32,768]{2,1,0:T(8,128)(2,1)S(1)} %get-tuple-element.75), channel_id=1, source_target_pairs={{128,192},{129,193},{130,194},{131,195},{132,196},{133,197},{134,1... | collective-permute-start | bytes 442376 | tf_op jit(solution)/shard_map/ppermute | solution.py:315
  30.3 1.3 %collective-permute-start.23 = (bf16[3,32,768]{2,1,0:T(8,128)(2,1)S(1)}, bf16[3,32,768]{2,1,0:T(8,128)(2,1)S(1)}, u32[]{:S(2)}, u32[]{:S(2)}) collective-permute-start(bf16[3,32,768]{2,1,0:T(8,128)(2,1)S(1)} %get-tuple-element.79), channel_id=1, source_target_pairs={{128,255},{131,196},{132,195},{135,200},{136,199},{139,204},{140,2... | collective-permute-start | bytes 442376 | tf_op jit(solution)/shard_map/ppermute | solution.py:316
  31.6 1.3 %collective-permute-start.21 = (bf16[5,32,768]{2,1,0:T(8,128)(2,1)S(1)}, bf16[5,32,768]{2,1,0:T(8,128)(2,1)S(1)}, u32[]{:S(2)}, u32[]{:S(2)}) collective-permute-start(bf16[5,32,768]{2,1,0:T(8,128)(2,1)S(1)} %get-tuple-element.78), channel_id=1, source_target_pairs={{128,192},{129,193},{130,194},{131,195},{132,196},{133,197},{134,1... | collective-permute-start | bytes 737288 | tf_op jit(solution)/shard_map/ppermute | solution.py:317
  33.5 35.5 %collective-permute-done.20.refs_1_ = bf16[3,32,768]{2,1,0:T(8,128)(2,1)S(1)} collective-permute-done((bf16[3,32,768]{2,1,0:T(8,128)(2,1)S(1)}, bf16[3,32,768]{2,1,0:T(8,128)(2,1)S(1)}, u32[]{:S(2)}, u32[]{:S(2)}) %collective-permute-start.20) | collective-permute-done | bytes 147488 | tf_op jit(solution)/shard_map/ppermute | solution.py:315
  69.1 1.3 %collective-permute-start.19 = (bf16[3,32,768]{2,1,0:T(8,128)(2,1)S(1)}, bf16[3,32,768]{2,1,0:T(8,128)(2,1)S(1)}, u32[]{:S(2)}, u32[]{:S(2)}) collective-permute-start(bf16[3,32,768]{2,1,0:T(8,128)(2,1)S(1)} %get-tuple-element.74), channel_id=1, source_target_pairs={{128,192},{129,193},{130,194},{131,195},{132,196},{133,197},{134,1... | collective-permute-start | bytes 442376 | tf_op jit(solution)/shard_map/ppermute | solution.py:315
  70.4 1.3 %collective-permute-start.26 = (bf16[3,32,768]{2,1,0:T(8,128)(2,1)S(1)}, bf16[3,32,768]{2,1,0:T(8,128)(2,1)S(1)}, u32[]{:S(2)}, u32[]{:S(2)}) collective-permute-start(bf16[3,32,768]{2,1,0:T(8,128)(2,1)S(1)} %get-tuple-element.82), channel_id=1, source_target_pairs={{128,255},{131,196},{132,195},{135,200},{136,199},{139,204},{140,2... | collective-permute-start | bytes 442376 | tf_op jit(solution)/shard_map/ppermute | solution.py:316
  71.7 2.5 %collective-permute-done.23.refs_4_ = bf16[3,32,768]{2,1,0:T(8,128)(2,1)S(1)} collective-permute-done((bf16[3,32,768]{2,1,0:T(8,128)(2,1)S(1)}, bf16[3,32,768]{2,1,0:T(8,128)(2,1)S(1)}, u32[]{:S(2)}, u32[]{:S(2)}) %collective-permute-start.23) | collective-permute-done | bytes 147488 | tf_op jit(solution)/shard_map/ppermute | solution.py:316
  74.2 1.3 %collective-permute-start.24 = (bf16[5,32,768]{2,1,0:T(8,128)(2,1)S(1)}, bf16[5,32,768]{2,1,0:T(8,128)(2,1)S(1)}, u32[]{:S(2)}, u32[]{:S(2)}) collective-permute-start(bf16[5,32,768]{2,1,0:T(8,128)(2,1)S(1)} %get-tuple-element.81), channel_id=1, source_target_pairs={{128,192},{129,193},{130,194},{131,195},{132,196},{133,197},{134,1... | collective-permute-start | bytes 737288 | tf_op jit(solution)/shard_map/ppermute | solution.py:317
  75.7 7.0 %block.14.refs_11_ = bf16[8,32,768]{2,1,0:T(8,128)(2,1)S(1)} custom-call(s32[2]{0:T(128)S(1)} %pad_add_fusion.refs_0_, bf16[3,32,768]{2,1,0:T(8,128)(2,1)S(1)} %collective-permute-done.20.refs_1_, bf16[5,32,768]{2,1,0:T(8,128)(2,1)S(1)} %collective-permute-done.21.refs_2_, bf16[3,32,768]{2,1,0:T(8,128)(2,1)S(1)} %collective-permute-done.22.refs_3_, ...), custom_call_target="tpu_custom_call" | custom-call | flops 8589934592 | bytes 1024 | tf_op jit(solution)/shard_map/block/pallas_call | solution.py:250
  82.7 0.9 collective-permute-done.19.refs_1_
  83.5 3.7 %collective-permute-done.26.refs_4_ = bf16[3,32,768]{2,1,0:T(8,128)(2,1)S(1)} collective-permute-done((bf16[3,32,768]{2,1,0:T(8,128)(2,1)S(1)}, bf16[3,32,768]{2,1,0:T(8,128)(2,1)S(1)}, u32[]{:S(2)}, u32[]{:S(2)}) %collective-permute-start.26) | collective-permute-done | bytes 147488 | tf_op jit(solution)/shard_map/ppermute | solution.py:316
  87.3 2.9 %collective-permute-done.24.refs_2_ = bf16[5,32,768]{2,1,0:T(8,128)(2,1)S(1)} collective-permute-done((bf16[5,32,768]{2,1,0:T(8,128)(2,1)S(1)}, bf16[5,32,768]{2,1,0:T(8,128)(2,1)S(1)}, u32[]{:S(2)}, u32[]{:S(2)}) %collective-permute-start.24) | collective-permute-done | bytes 245792 | tf_op jit(solution)/shard_map/ppermute | solution.py:317
  90.2 7.9 %block.15 = bf16[1,2,8,32,768]{4,3,2,1,0:T(8,128)(2,1)} custom-call(s32[2]{0:T(128)S(1)} %pad_add_fusion.refs_0_, bf16[3,32,768]{2,1,0:T(8,128)(2,1)S(1)} %collective-permute-done.19.refs_1_, bf16[5,32,768]{2,1,0:T(8,128)(2,1)S(1)} %collective-permute-done.24.refs_2_, ...), custom_call_target="tpu_custom_call", output_to_operand_aliasing={{}: (12, {})} | custom-call | flops 8589934592 | bytes 1024 | tf_op jit(solution)/shard_map/block/pallas_call | solution.py:250
  (44 shorter events, 9.5 us)
Async XLA Ops:
  2.0 13.8 %collective-permute-start.1 = (bf16[2,3,32,768]{3,2,1,0:T(8,128)(2,1)S(1)}, bf16[2,3,32,768]{3,2,1,0:T(8,128)(2,1)S(1)}, u32[]{:S(2)}, u32[]{:S(2)}) collective-permute-start(bf16[2,3,32,768]{3,2,1,0:T(8,128)(2,1)S(1)} %get-tuple-element.46), channel_id=1, source_target_pairs={{0,63},{3,4},{4,3},{7,8},{8,7},{11,12},{12,11},{15,16},{16,15},{19... | collective-permute-start | bytes 884744 | tf_op jit(solution)/shard_map/ppermute | solution.py:293
  11.5 6.9 %collective-permute-start = (bf16[3,32,768]{2,1,0:T(8,128)(2,1)S(1)}, bf16[3,32,768]{2,1,0:T(8,128)(2,1)S(1)}, u32[]{:S(2)}, u32[]{:S(2)}) collective-permute-start(bf16[3,32,768]{2,1,0:T(8,128)(2,1)S(1)} %get-tuple-element.44.refs_1_), channel_id=1, source_target_pairs={{0,1},{1,0},{2,3},{3,2},{4,5},{5,4},{6,7},{7,6},{8,9},{9,8},{10,11... | collective-permute-start | bytes 442376 | tf_op jit(solution)/shard_map/ppermute | solution.py:305
  16.4 2.6 %collective-permute-start.4 = (bf16[3,32,768]{2,1,0:T(8,128)(2,1)S(1)}, bf16[3,32,768]{2,1,0:T(8,128)(2,1)S(1)}, u32[]{:S(2)}, u32[]{:S(2)}) collective-permute-start(bf16[3,32,768]{2,1,0:T(8,128)(2,1)S(1)} %get-tuple-element.55), channel_id=1, source_target_pairs={{0,64},{1,65},{2,66},{3,67},{4,68},{5,69},{6,70},{7,71},{8,72},{9,... | collective-permute-start | bytes 442376 | tf_op jit(solution)/shard_map/ppermute | solution.py:315
  17.1 3.5 %collective-permute-start.7 = (bf16[3,32,768]{2,1,0:T(8,128)(2,1)S(1)}, bf16[3,32,768]{2,1,0:T(8,128)(2,1)S(1)}, u32[]{:S(2)}, u32[]{:S(2)}) collective-permute-start(bf16[3,32,768]{2,1,0:T(8,128)(2,1)S(1)} %get-tuple-element.59), channel_id=1, source_target_pairs={{0,127},{3,68},{4,67},{7,72},{8,71},{11,76},{12,75},{15,80},{16,79... | collective-permute-start | bytes 442376 | tf_op jit(solution)/shard_map/ppermute | solution.py:316
  17.8 3.5 %collective-permute-start.5 = (bf16[5,32,768]{2,1,0:T(8,128)(2,1)S(1)}, bf16[5,32,768]{2,1,0:T(8,128)(2,1)S(1)}, u32[]{:S(2)}, u32[]{:S(2)}) collective-permute-start(bf16[5,32,768]{2,1,0:T(8,128)(2,1)S(1)} %get-tuple-element.58), channel_id=1, source_target_pairs={{0,64},{1,65},{2,66},{3,67},{4,68},{5,69},{6,70},{7,71},{8,72},{9,... | collective-permute-start | bytes 737288 | tf_op jit(solution)/shard_map/ppermute | solution.py:317
  19.3 2.8 %collective-permute-start.3 = (bf16[3,32,768]{2,1,0:T(8,128)(2,1)S(1)}, bf16[3,32,768]{2,1,0:T(8,128)(2,1)S(1)}, u32[]{:S(2)}, u32[]{:S(2)}) collective-permute-start(bf16[3,32,768]{2,1,0:T(8,128)(2,1)S(1)} %get-tuple-element.54), channel_id=1, source_target_pairs={{0,64},{1,65},{2,66},{3,67},{4,68},{5,69},{6,70},{7,71},{8,72},{9,... | collective-permute-start | bytes 442376 | tf_op jit(solution)/shard_map/ppermute | solution.py:315
  19.9 4.1 %collective-permute-start.10 = (bf16[3,32,768]{2,1,0:T(8,128)(2,1)S(1)}, bf16[3,32,768]{2,1,0:T(8,128)(2,1)S(1)}, u32[]{:S(2)}, u32[]{:S(2)}) collective-permute-start(bf16[3,32,768]{2,1,0:T(8,128)(2,1)S(1)} %get-tuple-element.63), channel_id=1, source_target_pairs={{0,127},{3,68},{4,67},{7,72},{8,71},{11,76},{12,75},{15,80},{16,79... | collective-permute-start | bytes 442376 | tf_op jit(solution)/shard_map/ppermute | solution.py:316
  20.6 4.1 %collective-permute-start.8 = (bf16[5,32,768]{2,1,0:T(8,128)(2,1)S(1)}, bf16[5,32,768]{2,1,0:T(8,128)(2,1)S(1)}, u32[]{:S(2)}, u32[]{:S(2)}) collective-permute-start(bf16[5,32,768]{2,1,0:T(8,128)(2,1)S(1)} %get-tuple-element.62), channel_id=1, source_target_pairs={{0,64},{1,65},{2,66},{3,67},{4,68},{5,69},{6,70},{7,71},{8,72},{9,... | collective-permute-start | bytes 737288 | tf_op jit(solution)/shard_map/ppermute | solution.py:317
  22.1 2.6 %collective-permute-start.9 = (bf16[3,32,768]{2,1,0:T(8,128)(2,1)S(1)}, bf16[3,32,768]{2,1,0:T(8,128)(2,1)S(1)}, u32[]{:S(2)}, u32[]{:S(2)}) collective-permute-start(bf16[3,32,768]{2,1,0:T(8,128)(2,1)S(1)} %collective-permute-done.3.refs_1_), channel_id=1, source_target_pairs={{0,1},{1,0},{2,3},{3,2},{4,5},{5,4},{6,7},{7,6},{8,9},{9,8},{10,11... | collective-permute-start | bytes 442376 | tf_op jit(solution)/shard_map/ppermute | solution.py:305
  22.7 2.7 %collective-permute-start.12 = (bf16[3,32,768]{2,1,0:T(8,128)(2,1)S(1)}, bf16[3,32,768]{2,1,0:T(8,128)(2,1)S(1)}, u32[]{:S(2)}, u32[]{:S(2)}) collective-permute-start(bf16[3,32,768]{2,1,0:T(8,128)(2,1)S(1)} %get-tuple-element.65), channel_id=1, source_target_pairs={{64,128},{65,129},{66,130},{67,131},{68,132},{69,133},{70,134},{71... | collective-permute-start | bytes 442376 | tf_op jit(solution)/shard_map/ppermute | solution.py:315
  23.4 3.5 %collective-permute-start.15 = (bf16[3,32,768]{2,1,0:T(8,128)(2,1)S(1)}, bf16[3,32,768]{2,1,0:T(8,128)(2,1)S(1)}, u32[]{:S(2)}, u32[]{:S(2)}) collective-permute-start(bf16[3,32,768]{2,1,0:T(8,128)(2,1)S(1)} %get-tuple-element.69), channel_id=1, source_target_pairs={{64,191},{67,132},{68,131},{71,136},{72,135},{75,140},{76,139},{79... | collective-permute-start | bytes 442376 | tf_op jit(solution)/shard_map/ppermute | solution.py:316
  24.0 3.5 %collective-permute-start.13 = (bf16[5,32,768]{2,1,0:T(8,128)(2,1)S(1)}, bf16[5,32,768]{2,1,0:T(8,128)(2,1)S(1)}, u32[]{:S(2)}, u32[]{:S(2)}) collective-permute-start(bf16[5,32,768]{2,1,0:T(8,128)(2,1)S(1)} %get-tuple-element.68), channel_id=1, source_target_pairs={{64,128},{65,129},{66,130},{67,131},{68,132},{69,133},{70,134},{71... | collective-permute-start | bytes 737288 | tf_op jit(solution)/shard_map/ppermute | solution.py:317
  25.5 2.7 %collective-permute-start.11 = (bf16[3,32,768]{2,1,0:T(8,128)(2,1)S(1)}, bf16[3,32,768]{2,1,0:T(8,128)(2,1)S(1)}, u32[]{:S(2)}, u32[]{:S(2)}) collective-permute-start(bf16[3,32,768]{2,1,0:T(8,128)(2,1)S(1)} %get-tuple-element.64), channel_id=1, source_target_pairs={{64,128},{65,129},{66,130},{67,131},{68,132},{69,133},{70,134},{71... | collective-permute-start | bytes 442376 | tf_op jit(solution)/shard_map/ppermute | solution.py:315
  26.2 5.4 %collective-permute-start.18 = (bf16[3,32,768]{2,1,0:T(8,128)(2,1)S(1)}, bf16[3,32,768]{2,1,0:T(8,128)(2,1)S(1)}, u32[]{:S(2)}, u32[]{:S(2)}) collective-permute-start(bf16[3,32,768]{2,1,0:T(8,128)(2,1)S(1)} %get-tuple-element.73), channel_id=1, source_target_pairs={{64,191},{67,132},{68,131},{71,136},{72,135},{75,140},{76,139},{79... | collective-permute-start | bytes 442376 | tf_op jit(solution)/shard_map/ppermute | solution.py:316
  26.9 6.0 %collective-permute-start.16 = (bf16[5,32,768]{2,1,0:T(8,128)(2,1)S(1)}, bf16[5,32,768]{2,1,0:T(8,128)(2,1)S(1)}, u32[]{:S(2)}, u32[]{:S(2)}) collective-permute-start(bf16[5,32,768]{2,1,0:T(8,128)(2,1)S(1)} %get-tuple-element.72), channel_id=1, source_target_pairs={{64,128},{65,129},{66,130},{67,131},{68,132},{69,133},{70,134},{71... | collective-permute-start | bytes 737288 | tf_op jit(solution)/shard_map/ppermute | solution.py:317
  28.2 4.7 %collective-permute-start.17 = (bf16[3,32,768]{2,1,0:T(8,128)(2,1)S(1)}, bf16[3,32,768]{2,1,0:T(8,128)(2,1)S(1)}, u32[]{:S(2)}, u32[]{:S(2)}) collective-permute-start(bf16[3,32,768]{2,1,0:T(8,128)(2,1)S(1)} %collective-permute-done.11.refs_1_), channel_id=1, source_target_pairs={{0,1},{1,0},{2,3},{3,2},{4,5},{5,4},{6,7},{7,6},{8,9},{9,8},{10,11... | collective-permute-start | bytes 442376 | tf_op jit(solution)/shard_map/ppermute | solution.py:305
  29.0 40.0 %collective-permute-start.20 = (bf16[3,32,768]{2,1,0:T(8,128)(2,1)S(1)}, bf16[3,32,768]{2,1,0:T(8,128)(2,1)S(1)}, u32[]{:S(2)}, u32[]{:S(2)}) collective-permute-start(bf16[3,32,768]{2,1,0:T(8,128)(2,1)S(1)} %get-tuple-element.75), channel_id=1, source_target_pairs={{128,192},{129,193},{130,194},{131,195},{132,196},{133,197},{134,1... | collective-permute-start | bytes 442376 | tf_op jit(solution)/shard_map/ppermute | solution.py:315
  30.3 43.9 %collective-permute-start.23 = (bf16[3,32,768]{2,1,0:T(8,128)(2,1)S(1)}, bf16[3,32,768]{2,1,0:T(8,128)(2,1)S(1)}, u32[]{:S(2)}, u32[]{:S(2)}) collective-permute-start(bf16[3,32,768]{2,1,0:T(8,128)(2,1)S(1)} %get-tuple-element.79), channel_id=1, source_target_pairs={{128,255},{131,196},{132,195},{135,200},{136,199},{139,204},{140,2... | collective-permute-start | bytes 442376 | tf_op jit(solution)/shard_map/ppermute | solution.py:316
  31.6 44.1 %collective-permute-start.21 = (bf16[5,32,768]{2,1,0:T(8,128)(2,1)S(1)}, bf16[5,32,768]{2,1,0:T(8,128)(2,1)S(1)}, u32[]{:S(2)}, u32[]{:S(2)}) collective-permute-start(bf16[5,32,768]{2,1,0:T(8,128)(2,1)S(1)} %get-tuple-element.78), channel_id=1, source_target_pairs={{128,192},{129,193},{130,194},{131,195},{132,196},{133,197},{134,1... | collective-permute-start | bytes 737288 | tf_op jit(solution)/shard_map/ppermute | solution.py:317
  69.0 6.7 %collective-permute-start.22 = (bf16[3,32,768]{2,1,0:T(8,128)(2,1)S(1)}, bf16[3,32,768]{2,1,0:T(8,128)(2,1)S(1)}, u32[]{:S(2)}, u32[]{:S(2)}) collective-permute-start(bf16[3,32,768]{2,1,0:T(8,128)(2,1)S(1)} %collective-permute-done.20.refs_1_), channel_id=1, source_target_pairs={{0,1},{1,0},{2,3},{3,2},{4,5},{5,4},{6,7},{7,6},{8,9},{9,8},{10,11... | collective-permute-start | bytes 442376 | tf_op jit(solution)/shard_map/ppermute | solution.py:305
  69.1 14.5 %collective-permute-start.19 = (bf16[3,32,768]{2,1,0:T(8,128)(2,1)S(1)}, bf16[3,32,768]{2,1,0:T(8,128)(2,1)S(1)}, u32[]{:S(2)}, u32[]{:S(2)}) collective-permute-start(bf16[3,32,768]{2,1,0:T(8,128)(2,1)S(1)} %get-tuple-element.74), channel_id=1, source_target_pairs={{128,192},{129,193},{130,194},{131,195},{132,196},{133,197},{134,1... | collective-permute-start | bytes 442376 | tf_op jit(solution)/shard_map/ppermute | solution.py:315
  70.4 16.9 %collective-permute-start.26 = (bf16[3,32,768]{2,1,0:T(8,128)(2,1)S(1)}, bf16[3,32,768]{2,1,0:T(8,128)(2,1)S(1)}, u32[]{:S(2)}, u32[]{:S(2)}) collective-permute-start(bf16[3,32,768]{2,1,0:T(8,128)(2,1)S(1)} %get-tuple-element.82), channel_id=1, source_target_pairs={{128,255},{131,196},{132,195},{135,200},{136,199},{139,204},{140,2... | collective-permute-start | bytes 442376 | tf_op jit(solution)/shard_map/ppermute | solution.py:316
  74.2 16.0 %collective-permute-start.24 = (bf16[5,32,768]{2,1,0:T(8,128)(2,1)S(1)}, bf16[5,32,768]{2,1,0:T(8,128)(2,1)S(1)}, u32[]{:S(2)}, u32[]{:S(2)}) collective-permute-start(bf16[5,32,768]{2,1,0:T(8,128)(2,1)S(1)} %get-tuple-element.81), channel_id=1, source_target_pairs={{128,192},{129,193},{130,194},{131,195},{132,196},{133,197},{134,1... | collective-permute-start | bytes 737288 | tf_op jit(solution)/shard_map/ppermute | solution.py:317
  83.5 6.7 %collective-permute-start.25 = (bf16[3,32,768]{2,1,0:T(8,128)(2,1)S(1)}, bf16[3,32,768]{2,1,0:T(8,128)(2,1)S(1)}, u32[]{:S(2)}, u32[]{:S(2)}) collective-permute-start(bf16[3,32,768]{2,1,0:T(8,128)(2,1)S(1)} %collective-permute-done.19.refs_1_), channel_id=1, source_target_pairs={{0,1},{1,0},{2,3},{3,2},{4,5},{5,4},{6,7},{7,6},{8,9},{9,8},{10,11... | collective-permute-start | bytes 442376 | tf_op jit(solution)/shard_map/ppermute | solution.py:305
  (3 other events, 6.7 us)

commit v3 on v2

--- a/solution.py
+++ b/solution.py
@@ -31,34 +31,39 @@
     return copies
 
 
+def cross_kernel(flags, images, cross, sems):
+    micros, rows = images.shape[:2]
+    copies = []
+    for m in range(micros):
+        for row in range(rows - CROSS, rows):
+            copies.append((images.at[m, own_row(flags[1], rows, row)], cross.at[m, row - (rows - CROSS)]))
+    for copy in run_copies(copies, sems):
+        copy.wait()
+
+
 def rows_kernel(flags, images, *rest):
     micros, rows = images.shape[:2]
     sems = rest[-1]
     copies = []
     for m in range(micros):
-        near, far, cross = rest[m], rest[micros + m], rest[2 * micros]
+        near, far = rest[m], rest[micros + m]
         for row in range(rows):
             here = images.at[m, own_row(flags[1], rows, row)]
             copies.append((here, near.at[row] if row < NEAR else far.at[row - NEAR]))
-            if row >= rows - CROSS:
-                copies.append((here, cross.at[m, row - (rows - CROSS)]))
     for copy in run_copies(copies, sems):
         copy.wait()
 
 
-def mirrored_rows(flags, images):
-    micros, rows, width, channels = images.shape
+def mirrored_rows(kernel, name, flags, images, shapes, copies):
     return pl.pallas_call(
-        rows_kernel,
-        out_shape=[pltpu.VMEM((NEAR, width, channels), BF)] * micros
-        + [pltpu.VMEM((rows - NEAR, width, channels), BF)] * micros
-        + [pltpu.VMEM((micros, CROSS, width, channels), BF)],
+        kernel,
+        out_shape=[pltpu.VMEM(shape, BF) for shape in shapes],
         in_specs=[pl.BlockSpec(memory_space=pltpu.SMEM), pl.BlockSpec(memory_space=pltpu.HBM)],
-        out_specs=[pl.BlockSpec(memory_space=pltpu.VMEM)] * (2 * micros + 1),
-        scratch_shapes=[pltpu.SemaphoreType.DMA((micros * (rows + CROSS),))],
+        out_specs=[pl.BlockSpec(memory_space=pltpu.VMEM)] * len(shapes),
+        scratch_shapes=[pltpu.SemaphoreType.DMA((copies,))],
         compiler_params=pltpu.CompilerParams(vmem_limit_bytes=2**20),
-        cost_estimate=pl.CostEstimate(flops=0, bytes_accessed=2 * rows * width * channels, transcendentals=0),
-        name="mirrored_rows",
+        cost_estimate=pl.CostEstimate(flops=0, bytes_accessed=2**21, transcendentals=0),
+        name=name,
     )(flags, pltpu.with_memory_space_constraint(images, pltpu.HBM))
 
 
@@ -289,8 +294,11 @@
 
     same = {p: p for p in range(places)}
 
-    *parts, cross = mirrored_rows(flags[0], images)
+    shape = (micros, CROSS, width, channels)
+    cross = mirrored_rows(cross_kernel, "cross_rows", flags[0], images, [shape], micros * CROSS)[0]
     cross = lax.ppermute(cross, axes, near_pairs)
+    shapes = [(NEAR, width, channels)] * micros + [(rows - NEAR, width, channels)] * micros
+    parts = mirrored_rows(rows_kernel, "own_rows", flags[0], images, shapes, micros * rows)
     params = setup(flags[0], dw_weight, (dw_bias, ln_gain, ln_bias, b_out, layer_scale), b_in, width)
     weights = (w_in[0], w_out[0])
 

time: 98.8 us -> 98.5 us (level)
  waiting for transfers between devices: 47.9 us -> 46.1 us
  Pallas kernels: 22.2 us -> 23.6 us
    ppermute x1, waiting for transfers between devices: 2.17 us -> 0.36 us  [body(): cross = lax.ppermute(cross, axes, near_pairs)]
    pallas_call x1 -> x2, Pallas kernels: 1.95 us -> 3.32 us  [mirrored_rows(): pl.pallas_call(kernel, out_shape=[pltpu.VMEM(shape, BF) for shape in shap...]
  transfers between devices with their start and end apart: 27 -> 27, of which waited for: 7 -> 7; matrix products, arithmetic and copies ran while one was open for 0% -> 0% of each run, Pallas kernels for 13% -> 14%
where the time goes in v3:
time: 98.5 us; the launch traced here: 97.9 us
  waiting for transfers between devices  46.1 us (47%)
  starting transfers between devices  27.3 us (28%)
  Pallas kernels  23.6 us (24%)
    ppermute x6, waiting for transfers between devices, body(): near = lax.ppermute(relayed[0], axes, relay_pairs(section, same))  36.4 us
    pallas_call x8, Pallas kernels, run_block(): pl.pallas_call(functools.partial(block_kernel, micro, last, final, 768),...  18.6 us
    ppermute x1, starting transfers between devices, body(): cross = lax.ppermute(cross, axes, near_pairs)  9.4 us
    ppermute x6, waiting for transfers between devices, body(): cross = lax.ppermute(relayed[2], axes, relay_pairs(section, facing))  5.74 us
    ppermute x6, starting transfers between devices, body(): far = lax.ppermute(relayed[1], axes, relay_pairs(section, same))  5.28 us
    ppermute x6, starting transfers between devices, body(): cross = lax.ppermute(relayed[2], axes, relay_pairs(section, facing))  5.26 us
    ppermute x6, starting transfers between devices, body(): near = lax.ppermute(relayed[0], axes, relay_pairs(section, same))  5.21 us
    ppermute x6, waiting for transfers between devices, body(): far = lax.ppermute(relayed[1], axes, relay_pairs(section, same))  3.61 us
  transfers between devices with their start and end apart: 27, of which 7 were waited for; matrix products, arithmetic and copies ran while one was open for 0% of the time, Pallas kernels for 14%

profile of v3, /device:TPU:24, one launch (start us, length us, event | category | flops | bytes accessed | tf_op | source)
XLA Modules:
  0.0 97.9 jit_solution(5771827254997872242)
XLA Ops:
  0.1 1.5 %cross_rows.1 = bf16[2,3,32,768]{3,2,1,0:T(8,128)(2,1)S(1)} custom-call(s32[2]{0:T(128)S(1)} %pad_add_fusion.3.flags.refs_0_, bf16[2,8,32,768]{3,2,1,0:T(8,128)(2,1)} %images.3), custom_call_target="tpu_custom_call" | custom-call | bytes 2097152 | tf_op jit(solution)/shard_map/cross_rows/pallas_call | solution.py:58
  1.6 9.4 %collective-permute-start.1 = (bf16[2,3,32,768]{3,2,1,0:T(8,128)(2,1)S(1)}, bf16[2,3,32,768]{3,2,1,0:T(8,128)(2,1)S(1)}, u32[]{:S(2)}, u32[]{:S(2)}) collective-permute-start(bf16[2,3,32,768]{3,2,1,0:T(8,128)(2,1)S(1)} %cross_rows.1), channel_id=1, source_target_pairs={{0,63},{3,4},{4,3},{7,8},{8,7},{11,12},{12,11},{15,16},{16,15},{19... | collective-permute-start | bytes 884744 | tf_op jit(solution)/shard_map/ppermute | solution.py:299
  11.0 1.8 %own_rows.1 = (bf16[3,32,768]{2,1,0:T(8,128)(2,1)S(1)}, bf16[3,32,768]{2,1,0:T(8,128)(2,1)S(1)}, bf16[5,32,768]{2,1,0:T(8,128)(2,1)S(1)}, bf16[5,32,768]{2,1,0:T(8,128)(2,1)S(1)}) custom-call(s32[2]{0:T(128)S(1)} %pad_add_fusion.3.flags.refs_0_, bf16[2,8,32,768]{3,2,1,0:T(8,128)(2,1)} %images.3), custom_call_target="tpu_custom_call" | custom-call | bytes 2097152 | tf_op jit(solution)/shard_map/own_rows/pallas_call | solution.py:58
  13.4 1.6 %setup.1 = (bf16[49,16,768]{2,1,0:T(8,128)(2,1)S(1)}, f32[5,1,768]{2,1,0:T(1,128)S(1)}, f32[1,3072]{1,0:T(1,128)S(1)}, bf16[32,224]{1,0:T(8,128)(2,1)S(1)}) custom-call(s32[2]{0:T(128)S(1)} %pad_add_fusion.3.flags.refs_0_, bf16[1,7,7,768]{3,2,1,0:T(8,128)(2,1)} %weight.1, f32[1,768]{1,0:T(1,128)} %conv_bias.1, f32[1,768]{1,0:T(1,128)} %gain.1, ...), custom_call_target="tpu_custom_call" | custom-call | bytes 4194304 | tf_op jit(solution)/shard_map/setup/pallas_call | solution.py:94
  16.0 0.7 collective-permute-start.4
  17.3 0.7 collective-permute-start.5
  20.2 0.7 collective-permute-start.8
  20.9 0.8 block.10
  23.6 0.7 collective-permute-start.13
  26.5 0.7 collective-permute-start.16
  27.8 0.8 collective-permute-start.17
  28.6 1.3 %collective-permute-start.20 = (bf16[3,32,768]{2,1,0:T(8,128)(2,1)S(1)}, bf16[3,32,768]{2,1,0:T(8,128)(2,1)S(1)}, u32[]{:S(2)}, u32[]{:S(2)}) collective-permute-start(bf16[3,32,768]{2,1,0:T(8,128)(2,1)S(1)} %get-tuple-element.73), channel_id=1, source_target_pairs={{128,192},{129,193},{130,194},{131,195},{132,196},{133,197},{134,1... | collective-permute-start | bytes 442376 | tf_op jit(solution)/shard_map/ppermute | solution.py:323
  29.9 1.3 %collective-permute-start.23 = (bf16[3,32,768]{2,1,0:T(8,128)(2,1)S(1)}, bf16[3,32,768]{2,1,0:T(8,128)(2,1)S(1)}, u32[]{:S(2)}, u32[]{:S(2)}) collective-permute-start(bf16[3,32,768]{2,1,0:T(8,128)(2,1)S(1)} %get-tuple-element.77), channel_id=1, source_target_pairs={{128,255},{131,196},{132,195},{135,200},{136,199},{139,204},{140,2... | collective-permute-start | bytes 442376 | tf_op jit(solution)/shard_map/ppermute | solution.py:324
  31.2 1.3 %collective-permute-start.21 = (bf16[5,32,768]{2,1,0:T(8,128)(2,1)S(1)}, bf16[5,32,768]{2,1,0:T(8,128)(2,1)S(1)}, u32[]{:S(2)}, u32[]{:S(2)}) collective-permute-start(bf16[5,32,768]{2,1,0:T(8,128)(2,1)S(1)} %get-tuple-element.76), channel_id=1, source_target_pairs={{128,192},{129,193},{130,194},{131,195},{132,196},{133,197},{134,1... | collective-permute-start | bytes 737288 | tf_op jit(solution)/shard_map/ppermute | solution.py:325
  33.1 36.0 %collective-permute-done.20.refs_1_ = bf16[3,32,768]{2,1,0:T(8,128)(2,1)S(1)} collective-permute-done((bf16[3,32,768]{2,1,0:T(8,128)(2,1)S(1)}, bf16[3,32,768]{2,1,0:T(8,128)(2,1)S(1)}, u32[]{:S(2)}, u32[]{:S(2)}) %collective-permute-start.20) | collective-permute-done | bytes 147488 | tf_op jit(solution)/shard_map/ppermute | solution.py:323
  69.2 1.3 %collective-permute-start.19 = (bf16[3,32,768]{2,1,0:T(8,128)(2,1)S(1)}, bf16[3,32,768]{2,1,0:T(8,128)(2,1)S(1)}, u32[]{:S(2)}, u32[]{:S(2)}) collective-permute-start(bf16[3,32,768]{2,1,0:T(8,128)(2,1)S(1)} %get-tuple-element.72), channel_id=1, source_target_pairs={{128,192},{129,193},{130,194},{131,195},{132,196},{133,197},{134,1... | collective-permute-start | bytes 442376 | tf_op jit(solution)/shard_map/ppermute | solution.py:323
  70.5 1.3 %collective-permute-start.26 = (bf16[3,32,768]{2,1,0:T(8,128)(2,1)S(1)}, bf16[3,32,768]{2,1,0:T(8,128)(2,1)S(1)}, u32[]{:S(2)}, u32[]{:S(2)}) collective-permute-start(bf16[3,32,768]{2,1,0:T(8,128)(2,1)S(1)} %get-tuple-element.80), channel_id=1, source_target_pairs={{128,255},{131,196},{132,195},{135,200},{136,199},{139,204},{140,2... | collective-permute-start | bytes 442376 | tf_op jit(solution)/shard_map/ppermute | solution.py:324
  71.8 2.0 %collective-permute-done.23.refs_4_ = bf16[3,32,768]{2,1,0:T(8,128)(2,1)S(1)} collective-permute-done((bf16[3,32,768]{2,1,0:T(8,128)(2,1)S(1)}, bf16[3,32,768]{2,1,0:T(8,128)(2,1)S(1)}, u32[]{:S(2)}, u32[]{:S(2)}) %collective-permute-start.23) | collective-permute-done | bytes 147488 | tf_op jit(solution)/shard_map/ppermute | solution.py:324
  73.8 1.3 %collective-permute-start.24 = (bf16[5,32,768]{2,1,0:T(8,128)(2,1)S(1)}, bf16[5,32,768]{2,1,0:T(8,128)(2,1)S(1)}, u32[]{:S(2)}, u32[]{:S(2)}) collective-permute-start(bf16[5,32,768]{2,1,0:T(8,128)(2,1)S(1)} %get-tuple-element.79), channel_id=1, source_target_pairs={{128,192},{129,193},{130,194},{131,195},{132,196},{133,197},{134,1... | collective-permute-start | bytes 737288 | tf_op jit(solution)/shard_map/ppermute | solution.py:325
  75.1 0.7 collective-permute-done.21.refs_2_
  75.8 7.0 %block.14.refs_11_ = bf16[8,32,768]{2,1,0:T(8,128)(2,1)S(1)} custom-call(s32[2]{0:T(128)S(1)} %pad_add_fusion.refs_0_, bf16[3,32,768]{2,1,0:T(8,128)(2,1)S(1)} %collective-permute-done.20.refs_1_, bf16[5,32,768]{2,1,0:T(8,128)(2,1)S(1)} %collective-permute-done.21.refs_2_, bf16[3,32,768]{2,1,0:T(8,128)(2,1)S(1)} %collective-permute-done.22.refs_3_, ...), custom_call_target="tpu_custom_call" | custom-call | flops 8589934592 | bytes 1024 | tf_op jit(solution)/shard_map/block/pallas_call | solution.py:255
  83.1 3.7 %collective-permute-done.26.refs_4_ = bf16[3,32,768]{2,1,0:T(8,128)(2,1)S(1)} collective-permute-done((bf16[3,32,768]{2,1,0:T(8,128)(2,1)S(1)}, bf16[3,32,768]{2,1,0:T(8,128)(2,1)S(1)}, u32[]{:S(2)}, u32[]{:S(2)}) %collective-permute-start.26) | collective-permute-done | bytes 147488 | tf_op jit(solution)/shard_map/ppermute | solution.py:324
  86.9 2.9 %collective-permute-done.24.refs_2_ = bf16[5,32,768]{2,1,0:T(8,128)(2,1)S(1)} collective-permute-done((bf16[5,32,768]{2,1,0:T(8,128)(2,1)S(1)}, bf16[5,32,768]{2,1,0:T(8,128)(2,1)S(1)}, u32[]{:S(2)}, u32[]{:S(2)}) %collective-permute-start.24) | collective-permute-done | bytes 245792 | tf_op jit(solution)/shard_map/ppermute | solution.py:325
  89.8 7.9 %block.15 = bf16[1,2,8,32,768]{4,3,2,1,0:T(8,128)(2,1)} custom-call(s32[2]{0:T(128)S(1)} %pad_add_fusion.refs_0_, bf16[3,32,768]{2,1,0:T(8,128)(2,1)S(1)} %collective-permute-done.19.refs_1_, bf16[5,32,768]{2,1,0:T(8,128)(2,1)S(1)} %collective-permute-done.24.refs_2_, ...), custom_call_target="tpu_custom_call", output_to_operand_aliasing={{}: (12, {})} | custom-call | flops 8589934592 | bytes 1024 | tf_op jit(solution)/shard_map/block/pallas_call | solution.py:255
  (45 shorter events, 10.0 us)
Async XLA Ops:
  1.6 13.8 %collective-permute-start.1 = (bf16[2,3,32,768]{3,2,1,0:T(8,128)(2,1)S(1)}, bf16[2,3,32,768]{3,2,1,0:T(8,128)(2,1)S(1)}, u32[]{:S(2)}, u32[]{:S(2)}) collective-permute-start(bf16[2,3,32,768]{3,2,1,0:T(8,128)(2,1)S(1)} %cross_rows.1), channel_id=1, source_target_pairs={{0,63},{3,4},{4,3},{7,8},{8,7},{11,12},{12,11},{15,16},{16,15},{19... | collective-permute-start | bytes 884744 | tf_op jit(solution)/shard_map/ppermute | solution.py:299
  12.9 5.1 %collective-permute-start = (bf16[3,32,768]{2,1,0:T(8,128)(2,1)S(1)}, bf16[3,32,768]{2,1,0:T(8,128)(2,1)S(1)}, u32[]{:S(2)}, u32[]{:S(2)}) collective-permute-start(bf16[3,32,768]{2,1,0:T(8,128)(2,1)S(1)} %get-tuple-element.43.refs_1_), channel_id=1, source_target_pairs={{0,1},{1,0},{2,3},{3,2},{4,5},{5,4},{6,7},{7,6},{8,9},{9,8},{10,11... | collective-permute-start | bytes 442376 | tf_op jit(solution)/shard_map/ppermute | solution.py:313
  16.0 2.6 %collective-permute-start.4 = (bf16[3,32,768]{2,1,0:T(8,128)(2,1)S(1)}, bf16[3,32,768]{2,1,0:T(8,128)(2,1)S(1)}, u32[]{:S(2)}, u32[]{:S(2)}) collective-permute-start(bf16[3,32,768]{2,1,0:T(8,128)(2,1)S(1)} %get-tuple-element.53), channel_id=1, source_target_pairs={{0,64},{1,65},{2,66},{3,67},{4,68},{5,69},{6,70},{7,71},{8,72},{9,... | collective-permute-start | bytes 442376 | tf_op jit(solution)/shard_map/ppermute | solution.py:323
  16.7 3.5 %collective-permute-start.7 = (bf16[3,32,768]{2,1,0:T(8,128)(2,1)S(1)}, bf16[3,32,768]{2,1,0:T(8,128)(2,1)S(1)}, u32[]{:S(2)}, u32[]{:S(2)}) collective-permute-start(bf16[3,32,768]{2,1,0:T(8,128)(2,1)S(1)} %get-tuple-element.57), channel_id=1, source_target_pairs={{0,127},{3,68},{4,67},{7,72},{8,71},{11,76},{12,75},{15,80},{16,79... | collective-permute-start | bytes 442376 | tf_op jit(solution)/shard_map/ppermute | solution.py:324
  17.3 3.5 %collective-permute-start.5 = (bf16[5,32,768]{2,1,0:T(8,128)(2,1)S(1)}, bf16[5,32,768]{2,1,0:T(8,128)(2,1)S(1)}, u32[]{:S(2)}, u32[]{:S(2)}) collective-permute-start(bf16[5,32,768]{2,1,0:T(8,128)(2,1)S(1)} %get-tuple-element.56), channel_id=1, source_target_pairs={{0,64},{1,65},{2,66},{3,67},{4,68},{5,69},{6,70},{7,71},{8,72},{9,... | collective-permute-start | bytes 737288 | tf_op jit(solution)/shard_map/ppermute | solution.py:325
  18.8 2.8 %collective-permute-start.3 = (bf16[3,32,768]{2,1,0:T(8,128)(2,1)S(1)}, bf16[3,32,768]{2,1,0:T(8,128)(2,1)S(1)}, u32[]{:S(2)}, u32[]{:S(2)}) collective-permute-start(bf16[3,32,768]{2,1,0:T(8,128)(2,1)S(1)} %get-tuple-element.52), channel_id=1, source_target_pairs={{0,64},{1,65},{2,66},{3,67},{4,68},{5,69},{6,70},{7,71},{8,72},{9,... | collective-permute-start | bytes 442376 | tf_op jit(solution)/shard_map/ppermute | solution.py:323
  19.5 4.1 %collective-permute-start.10 = (bf16[3,32,768]{2,1,0:T(8,128)(2,1)S(1)}, bf16[3,32,768]{2,1,0:T(8,128)(2,1)S(1)}, u32[]{:S(2)}, u32[]{:S(2)}) collective-permute-start(bf16[3,32,768]{2,1,0:T(8,128)(2,1)S(1)} %get-tuple-element.61), channel_id=1, source_target_pairs={{0,127},{3,68},{4,67},{7,72},{8,71},{11,76},{12,75},{15,80},{16,79... | collective-permute-start | bytes 442376 | tf_op jit(solution)/shard_map/ppermute | solution.py:324
  20.2 4.1 %collective-permute-start.8 = (bf16[5,32,768]{2,1,0:T(8,128)(2,1)S(1)}, bf16[5,32,768]{2,1,0:T(8,128)(2,1)S(1)}, u32[]{:S(2)}, u32[]{:S(2)}) collective-permute-start(bf16[5,32,768]{2,1,0:T(8,128)(2,1)S(1)} %get-tuple-element.60), channel_id=1, source_target_pairs={{0,64},{1,65},{2,66},{3,67},{4,68},{5,69},{6,70},{7,71},{8,72},{9,... | collective-permute-start | bytes 737288 | tf_op jit(solution)/shard_map/ppermute | solution.py:325
  21.7 2.6 %collective-permute-start.9 = (bf16[3,32,768]{2,1,0:T(8,128)(2,1)S(1)}, bf16[3,32,768]{2,1,0:T(8,128)(2,1)S(1)}, u32[]{:S(2)}, u32[]{:S(2)}) collective-permute-start(bf16[3,32,768]{2,1,0:T(8,128)(2,1)S(1)} %collective-permute-done.3.refs_1_), channel_id=1, source_target_pairs={{0,1},{1,0},{2,3},{3,2},{4,5},{5,4},{6,7},{7,6},{8,9},{9,8},{10,11... | collective-permute-start | bytes 442376 | tf_op jit(solution)/shard_map/ppermute | solution.py:313
  22.3 2.7 %collective-permute-start.12 = (bf16[3,32,768]{2,1,0:T(8,128)(2,1)S(1)}, bf16[3,32,768]{2,1,0:T(8,128)(2,1)S(1)}, u32[]{:S(2)}, u32[]{:S(2)}) collective-permute-start(bf16[3,32,768]{2,1,0:T(8,128)(2,1)S(1)} %get-tuple-element.63), channel_id=1, source_target_pairs={{64,128},{65,129},{66,130},{67,131},{68,132},{69,133},{70,134},{71... | collective-permute-start | bytes 442376 | tf_op jit(solution)/shard_map/ppermute | solution.py:323
  22.9 3.5 %collective-permute-start.15 = (bf16[3,32,768]{2,1,0:T(8,128)(2,1)S(1)}, bf16[3,32,768]{2,1,0:T(8,128)(2,1)S(1)}, u32[]{:S(2)}, u32[]{:S(2)}) collective-permute-start(bf16[3,32,768]{2,1,0:T(8,128)(2,1)S(1)} %get-tuple-element.67), channel_id=1, source_target_pairs={{64,191},{67,132},{68,131},{71,136},{72,135},{75,140},{76,139},{79... | collective-permute-start | bytes 442376 | tf_op jit(solution)/shard_map/ppermute | solution.py:324
  23.6 3.5 %collective-permute-start.13 = (bf16[5,32,768]{2,1,0:T(8,128)(2,1)S(1)}, bf16[5,32,768]{2,1,0:T(8,128)(2,1)S(1)}, u32[]{:S(2)}, u32[]{:S(2)}) collective-permute-start(bf16[5,32,768]{2,1,0:T(8,128)(2,1)S(1)} %get-tuple-element.66), channel_id=1, source_target_pairs={{64,128},{65,129},{66,130},{67,131},{68,132},{69,133},{70,134},{71... | collective-permute-start | bytes 737288 | tf_op jit(solution)/shard_map/ppermute | solution.py:325
  25.1 2.7 %collective-permute-start.11 = (bf16[3,32,768]{2,1,0:T(8,128)(2,1)S(1)}, bf16[3,32,768]{2,1,0:T(8,128)(2,1)S(1)}, u32[]{:S(2)}, u32[]{:S(2)}) collective-permute-start(bf16[3,32,768]{2,1,0:T(8,128)(2,1)S(1)} %get-tuple-element.62), channel_id=1, source_target_pairs={{64,128},{65,129},{66,130},{67,131},{68,132},{69,133},{70,134},{71... | collective-permute-start | bytes 442376 | tf_op jit(solution)/shard_map/ppermute | solution.py:323
  25.8 5.4 %collective-permute-start.18 = (bf16[3,32,768]{2,1,0:T(8,128)(2,1)S(1)}, bf16[3,32,768]{2,1,0:T(8,128)(2,1)S(1)}, u32[]{:S(2)}, u32[]{:S(2)}) collective-permute-start(bf16[3,32,768]{2,1,0:T(8,128)(2,1)S(1)} %get-tuple-element.71), channel_id=1, source_target_pairs={{64,191},{67,132},{68,131},{71,136},{72,135},{75,140},{76,139},{79... | collective-permute-start | bytes 442376 | tf_op jit(solution)/shard_map/ppermute | solution.py:324
  26.5 6.0 %collective-permute-start.16 = (bf16[5,32,768]{2,1,0:T(8,128)(2,1)S(1)}, bf16[5,32,768]{2,1,0:T(8,128)(2,1)S(1)}, u32[]{:S(2)}, u32[]{:S(2)}) collective-permute-start(bf16[5,32,768]{2,1,0:T(8,128)(2,1)S(1)} %get-tuple-element.70), channel_id=1, source_target_pairs={{64,128},{65,129},{66,130},{67,131},{68,132},{69,133},{70,134},{71... | collective-permute-start | bytes 737288 | tf_op jit(solution)/shard_map/ppermute | solution.py:325
  27.8 4.7 %collective-permute-start.17 = (bf16[3,32,768]{2,1,0:T(8,128)(2,1)S(1)}, bf16[3,32,768]{2,1,0:T(8,128)(2,1)S(1)}, u32[]{:S(2)}, u32[]{:S(2)}) collective-permute-start(bf16[3,32,768]{2,1,0:T(8,128)(2,1)S(1)} %collective-permute-done.11.refs_1_), channel_id=1, source_target_pairs={{0,1},{1,0},{2,3},{3,2},{4,5},{5,4},{6,7},{7,6},{8,9},{9,8},{10,11... | collective-permute-start | bytes 442376 | tf_op jit(solution)/shard_map/ppermute | solution.py:313
  28.6 40.5 %collective-permute-start.20 = (bf16[3,32,768]{2,1,0:T(8,128)(2,1)S(1)}, bf16[3,32,768]{2,1,0:T(8,128)(2,1)S(1)}, u32[]{:S(2)}, u32[]{:S(2)}) collective-permute-start(bf16[3,32,768]{2,1,0:T(8,128)(2,1)S(1)} %get-tuple-element.73), channel_id=1, source_target_pairs={{128,192},{129,193},{130,194},{131,195},{132,196},{133,197},{134,1... | collective-permute-start | bytes 442376 | tf_op jit(solution)/shard_map/ppermute | solution.py:323
  29.9 43.9 %collective-permute-start.23 = (bf16[3,32,768]{2,1,0:T(8,128)(2,1)S(1)}, bf16[3,32,768]{2,1,0:T(8,128)(2,1)S(1)}, u32[]{:S(2)}, u32[]{:S(2)}) collective-permute-start(bf16[3,32,768]{2,1,0:T(8,128)(2,1)S(1)} %get-tuple-element.77), channel_id=1, source_target_pairs={{128,255},{131,196},{132,195},{135,200},{136,199},{139,204},{140,2... | collective-permute-start | bytes 442376 | tf_op jit(solution)/shard_map/ppermute | solution.py:324
  31.2 44.6 %collective-permute-start.21 = (bf16[5,32,768]{2,1,0:T(8,128)(2,1)S(1)}, bf16[5,32,768]{2,1,0:T(8,128)(2,1)S(1)}, u32[]{:S(2)}, u32[]{:S(2)}) collective-permute-start(bf16[5,32,768]{2,1,0:T(8,128)(2,1)S(1)} %get-tuple-element.76), channel_id=1, source_target_pairs={{128,192},{129,193},{130,194},{131,195},{132,196},{133,197},{134,1... | collective-permute-start | bytes 737288 | tf_op jit(solution)/shard_map/ppermute | solution.py:325
  69.1 6.6 %collective-permute-start.22 = (bf16[3,32,768]{2,1,0:T(8,128)(2,1)S(1)}, bf16[3,32,768]{2,1,0:T(8,128)(2,1)S(1)}, u32[]{:S(2)}, u32[]{:S(2)}) collective-permute-start(bf16[3,32,768]{2,1,0:T(8,128)(2,1)S(1)} %collective-permute-done.20.refs_1_), channel_id=1, source_target_pairs={{0,1},{1,0},{2,3},{3,2},{4,5},{5,4},{6,7},{7,6},{8,9},{9,8},{10,11... | collective-permute-start | bytes 442376 | tf_op jit(solution)/shard_map/ppermute | solution.py:313
  69.2 13.9 %collective-permute-start.19 = (bf16[3,32,768]{2,1,0:T(8,128)(2,1)S(1)}, bf16[3,32,768]{2,1,0:T(8,128)(2,1)S(1)}, u32[]{:S(2)}, u32[]{:S(2)}) collective-permute-start(bf16[3,32,768]{2,1,0:T(8,128)(2,1)S(1)} %get-tuple-element.72), channel_id=1, source_target_pairs={{128,192},{129,193},{130,194},{131,195},{132,196},{133,197},{134,1... | collective-permute-start | bytes 442376 | tf_op jit(solution)/shard_map/ppermute | solution.py:323
  70.5 16.4 %collective-permute-start.26 = (bf16[3,32,768]{2,1,0:T(8,128)(2,1)S(1)}, bf16[3,32,768]{2,1,0:T(8,128)(2,1)S(1)}, u32[]{:S(2)}, u32[]{:S(2)}) collective-permute-start(bf16[3,32,768]{2,1,0:T(8,128)(2,1)S(1)} %get-tuple-element.80), channel_id=1, source_target_pairs={{128,255},{131,196},{132,195},{135,200},{136,199},{139,204},{140,2... | collective-permute-start | bytes 442376 | tf_op jit(solution)/shard_map/ppermute | solution.py:324
  73.8 16.0 %collective-permute-start.24 = (bf16[5,32,768]{2,1,0:T(8,128)(2,1)S(1)}, bf16[5,32,768]{2,1,0:T(8,128)(2,1)S(1)}, u32[]{:S(2)}, u32[]{:S(2)}) collective-permute-start(bf16[5,32,768]{2,1,0:T(8,128)(2,1)S(1)} %get-tuple-element.79), channel_id=1, source_target_pairs={{128,192},{129,193},{130,194},{131,195},{132,196},{133,197},{134,1... | collective-permute-start | bytes 737288 | tf_op jit(solution)/shard_map/ppermute | solution.py:325
  83.1 6.7 %collective-permute-start.25 = (bf16[3,32,768]{2,1,0:T(8,128)(2,1)S(1)}, bf16[3,32,768]{2,1,0:T(8,128)(2,1)S(1)}, u32[]{:S(2)}, u32[]{:S(2)}) collective-permute-start(bf16[3,32,768]{2,1,0:T(8,128)(2,1)S(1)} %collective-permute-done.19.refs_1_), channel_id=1, source_target_pairs={{0,1},{1,0},{2,3},{3,2},{4,5},{5,4},{6,7},{7,6},{8,9},{9,8},{10,11... | collective-permute-start | bytes 442376 | tf_op jit(solution)/shard_map/ppermute | solution.py:313
  (3 other events, 6.7 us)

commit v4 on v3

--- a/solution.py
+++ b/solution.py
@@ -260,7 +260,7 @@
         scratch_shapes=scratch + [pltpu.SemaphoreType.DMA((4,))],
         input_output_aliases=aliases,
         compiler_params=pltpu.CompilerParams(vmem_limit_bytes=32 * 2**20),
-        cost_estimate=pl.CostEstimate(flops=2**33 if last else 2**33, bytes_accessed=2**10, transcendentals=0),
+        cost_estimate=pl.CostEstimate(flops=2**20 if last else 2**33, bytes_accessed=2**10, transcendentals=0),
         name="block",
     )(*operands)
     return relayed, kept

time: 98.5 us -> 98.5 us (level)
  transfers between devices with their start and end apart: 27 -> 27, of which waited for: 7 -> 6; matrix products, arithmetic and copies ran while one was open for 0% -> 0% of each run, Pallas kernels for 14% -> 14%
where the time goes in v4:
time: 98.5 us; the launch traced here: 97.9 us
  waiting for transfers between devices  46 us (47%)
  starting transfers between devices  27.4 us (28%)
  Pallas kernels  23.6 us (24%)
    ppermute x6, waiting for transfers between devices, body(): near = lax.ppermute(relayed[0], axes, relay_pairs(section, same))  36.8 us
    pallas_call x8, Pallas kernels, run_block(): pl.pallas_call(functools.partial(block_kernel, micro, last, final, 768),...  18.6 us
    ppermute x1, starting transfers between devices, body(): cross = lax.ppermute(cross, axes, near_pairs)  9.4 us
    ppermute x6, waiting for transfers between devices, body(): cross = lax.ppermute(relayed[2], axes, relay_pairs(section, facing))  5.83 us
    ppermute x6, starting transfers between devices, body(): far = lax.ppermute(relayed[1], axes, relay_pairs(section, same))  5.28 us
    ppermute x6, starting transfers between devices, body(): cross = lax.ppermute(relayed[2], axes, relay_pairs(section, facing))  5.26 us
    ppermute x6, starting transfers between devices, body(): near = lax.ppermute(relayed[0], axes, relay_pairs(section, same))  5.21 us
    pallas_call x2, Pallas kernels, mirrored_rows(): pl.pallas_call(kernel, out_shape=[pltpu.VMEM(shape, BF) for shape in shap...  3.32 us
  transfers between devices with their start and end apart: 27, of which 6 were waited for; matrix products, arithmetic and copies ran while one was open for 0% of the time, Pallas kernels for 14%

profile of v4, /device:TPU:24, one launch (start us, length us, event | category | flops | bytes accessed | tf_op | source)
XLA Modules:
  0.0 97.9 jit_solution(17759695386621122798)
XLA Ops:
  0.1 1.5 %cross_rows.1 = bf16[2,3,32,768]{3,2,1,0:T(8,128)(2,1)S(1)} custom-call(s32[2]{0:T(128)S(1)} %pad_add_fusion.3.flags.refs_0_, bf16[2,8,32,768]{3,2,1,0:T(8,128)(2,1)} %images.3), custom_call_target="tpu_custom_call" | custom-call | bytes 2097152 | tf_op jit(solution)/shard_map/cross_rows/pallas_call | solution.py:58
  1.6 9.4 %collective-permute-start.1 = (bf16[2,3,32,768]{3,2,1,0:T(8,128)(2,1)S(1)}, bf16[2,3,32,768]{3,2,1,0:T(8,128)(2,1)S(1)}, u32[]{:S(2)}, u32[]{:S(2)}) collective-permute-start(bf16[2,3,32,768]{3,2,1,0:T(8,128)(2,1)S(1)} %cross_rows.1), channel_id=1, source_target_pairs={{0,63},{3,4},{4,3},{7,8},{8,7},{11,12},{12,11},{15,16},{16,15},{19... | collective-permute-start | bytes 884744 | tf_op jit(solution)/shard_map/ppermute | solution.py:299
  11.0 1.8 %own_rows.1 = (bf16[3,32,768]{2,1,0:T(8,128)(2,1)S(1)}, bf16[3,32,768]{2,1,0:T(8,128)(2,1)S(1)}, bf16[5,32,768]{2,1,0:T(8,128)(2,1)S(1)}, bf16[5,32,768]{2,1,0:T(8,128)(2,1)S(1)}) custom-call(s32[2]{0:T(128)S(1)} %pad_add_fusion.3.flags.refs_0_, bf16[2,8,32,768]{3,2,1,0:T(8,128)(2,1)} %images.3), custom_call_target="tpu_custom_call" | custom-call | bytes 2097152 | tf_op jit(solution)/shard_map/own_rows/pallas_call | solution.py:58
  13.4 1.6 %setup.1 = (bf16[49,16,768]{2,1,0:T(8,128)(2,1)S(1)}, f32[5,1,768]{2,1,0:T(1,128)S(1)}, f32[1,3072]{1,0:T(1,128)S(1)}, bf16[32,224]{1,0:T(8,128)(2,1)S(1)}) custom-call(s32[2]{0:T(128)S(1)} %pad_add_fusion.3.flags.refs_0_, bf16[1,7,7,768]{3,2,1,0:T(8,128)(2,1)} %weight.1, f32[1,768]{1,0:T(1,128)} %conv_bias.1, f32[1,768]{1,0:T(1,128)} %gain.1, ...), custom_call_target="tpu_custom_call" | custom-call | bytes 4194304 | tf_op jit(solution)/shard_map/setup/pallas_call | solution.py:94
  16.0 0.7 collective-permute-start.4
  16.7 0.7 collective-permute-start.5
  17.4 0.7 collective-permute-start.7
  20.2 0.7 collective-permute-start.8
  20.9 0.8 block.10
  22.9 0.7 collective-permute-start.13
  26.5 0.7 collective-permute-start.16
  27.8 0.8 collective-permute-start.17
  28.6 1.3 %collective-permute-start.20 = (bf16[3,32,768]{2,1,0:T(8,128)(2,1)S(1)}, bf16[3,32,768]{2,1,0:T(8,128)(2,1)S(1)}, u32[]{:S(2)}, u32[]{:S(2)}) collective-permute-start(bf16[3,32,768]{2,1,0:T(8,128)(2,1)S(1)} %get-tuple-element.73), channel_id=1, source_target_pairs={{128,192},{129,193},{130,194},{131,195},{132,196},{133,197},{134,1... | collective-permute-start | bytes 442376 | tf_op jit(solution)/shard_map/ppermute | solution.py:323
  29.9 1.3 %collective-permute-start.21 = (bf16[5,32,768]{2,1,0:T(8,128)(2,1)S(1)}, bf16[5,32,768]{2,1,0:T(8,128)(2,1)S(1)}, u32[]{:S(2)}, u32[]{:S(2)}) collective-permute-start(bf16[5,32,768]{2,1,0:T(8,128)(2,1)S(1)} %get-tuple-element.76), channel_id=1, source_target_pairs={{128,192},{129,193},{130,194},{131,195},{132,196},{133,197},{134,1... | collective-permute-start | bytes 737288 | tf_op jit(solution)/shard_map/ppermute | solution.py:325
  31.2 1.3 %collective-permute-start.23 = (bf16[3,32,768]{2,1,0:T(8,128)(2,1)S(1)}, bf16[3,32,768]{2,1,0:T(8,128)(2,1)S(1)}, u32[]{:S(2)}, u32[]{:S(2)}) collective-permute-start(bf16[3,32,768]{2,1,0:T(8,128)(2,1)S(1)} %get-tuple-element.77), channel_id=1, source_target_pairs={{128,255},{131,196},{132,195},{135,200},{136,199},{139,204},{140,2... | collective-permute-start | bytes 442376 | tf_op jit(solution)/shard_map/ppermute | solution.py:324
  33.1 36.7 %collective-permute-done.20.refs_1_ = bf16[3,32,768]{2,1,0:T(8,128)(2,1)S(1)} collective-permute-done((bf16[3,32,768]{2,1,0:T(8,128)(2,1)S(1)}, bf16[3,32,768]{2,1,0:T(8,128)(2,1)S(1)}, u32[]{:S(2)}, u32[]{:S(2)}) %collective-permute-start.20) | collective-permute-done | bytes 147488 | tf_op jit(solution)/shard_map/ppermute | solution.py:323
  69.9 1.3 %collective-permute-start.19 = (bf16[3,32,768]{2,1,0:T(8,128)(2,1)S(1)}, bf16[3,32,768]{2,1,0:T(8,128)(2,1)S(1)}, u32[]{:S(2)}, u32[]{:S(2)}) collective-permute-start(bf16[3,32,768]{2,1,0:T(8,128)(2,1)S(1)} %get-tuple-element.72), channel_id=1, source_target_pairs={{128,192},{129,193},{130,194},{131,195},{132,196},{133,197},{134,1... | collective-permute-start | bytes 442376 | tf_op jit(solution)/shard_map/ppermute | solution.py:323
  71.2 1.3 %collective-permute-start.26 = (bf16[3,32,768]{2,1,0:T(8,128)(2,1)S(1)}, bf16[3,32,768]{2,1,0:T(8,128)(2,1)S(1)}, u32[]{:S(2)}, u32[]{:S(2)}) collective-permute-start(bf16[3,32,768]{2,1,0:T(8,128)(2,1)S(1)} %get-tuple-element.80), channel_id=1, source_target_pairs={{128,255},{131,196},{132,195},{135,200},{136,199},{139,204},{140,2... | collective-permute-start | bytes 442376 | tf_op jit(solution)/shard_map/ppermute | solution.py:324
  72.5 2.6 %collective-permute-done.23.refs_4_ = bf16[3,32,768]{2,1,0:T(8,128)(2,1)S(1)} collective-permute-done((bf16[3,32,768]{2,1,0:T(8,128)(2,1)S(1)}, bf16[3,32,768]{2,1,0:T(8,128)(2,1)S(1)}, u32[]{:S(2)}, u32[]{:S(2)}) %collective-permute-start.23) | collective-permute-done | bytes 147488 | tf_op jit(solution)/shard_map/ppermute | solution.py:324
  75.1 1.3 %collective-permute-start.24 = (bf16[5,32,768]{2,1,0:T(8,128)(2,1)S(1)}, bf16[5,32,768]{2,1,0:T(8,128)(2,1)S(1)}, u32[]{:S(2)}, u32[]{:S(2)}) collective-permute-start(bf16[5,32,768]{2,1,0:T(8,128)(2,1)S(1)} %get-tuple-element.79), channel_id=1, source_target_pairs={{128,192},{129,193},{130,194},{131,195},{132,196},{133,197},{134,1... | collective-permute-start | bytes 737288 | tf_op jit(solution)/shard_map/ppermute | solution.py:325
  76.5 7.0 %block.14.refs_11_ = bf16[8,32,768]{2,1,0:T(8,128)(2,1)S(1)} custom-call(s32[2]{0:T(128)S(1)} %pad_add_fusion.refs_0_, bf16[3,32,768]{2,1,0:T(8,128)(2,1)S(1)} %collective-permute-done.20.refs_1_, bf16[5,32,768]{2,1,0:T(8,128)(2,1)S(1)} %collective-permute-done.21.refs_2_, bf16[3,32,768]{2,1,0:T(8,128)(2,1)S(1)} %collective-permute-done.22.refs_3_, ...), custom_call_target="tpu_custom_call" | custom-call | flops 8589934592 | bytes 1024 | tf_op jit(solution)/shard_map/block/pallas_call | solution.py:255
  83.6 3.3 %collective-permute-done.26.refs_4_ = bf16[3,32,768]{2,1,0:T(8,128)(2,1)S(1)} collective-permute-done((bf16[3,32,768]{2,1,0:T(8,128)(2,1)S(1)}, bf16[3,32,768]{2,1,0:T(8,128)(2,1)S(1)}, u32[]{:S(2)}, u32[]{:S(2)}) %collective-permute-start.26) | collective-permute-done | bytes 147488 | tf_op jit(solution)/shard_map/ppermute | solution.py:324
  86.8 2.9 %collective-permute-done.24.refs_2_ = bf16[5,32,768]{2,1,0:T(8,128)(2,1)S(1)} collective-permute-done((bf16[5,32,768]{2,1,0:T(8,128)(2,1)S(1)}, bf16[5,32,768]{2,1,0:T(8,128)(2,1)S(1)}, u32[]{:S(2)}, u32[]{:S(2)}) %collective-permute-start.24) | collective-permute-done | bytes 245792 | tf_op jit(solution)/shard_map/ppermute | solution.py:325
  89.7 7.9 %block.15 = bf16[1,2,8,32,768]{4,3,2,1,0:T(8,128)(2,1)} custom-call(s32[2]{0:T(128)S(1)} %pad_add_fusion.refs_0_, bf16[3,32,768]{2,1,0:T(8,128)(2,1)S(1)} %collective-permute-done.19.refs_1_, bf16[5,32,768]{2,1,0:T(8,128)(2,1)S(1)} %collective-permute-done.24.refs_2_, ...), custom_call_target="tpu_custom_call", output_to_operand_aliasing={{}: (12, {})} | custom-call | flops 1048576 | bytes 1024 | tf_op jit(solution)/shard_map/block/pallas_call | solution.py:255
  (45 shorter events, 9.2 us)
Async XLA Ops:
  1.6 13.8 %collective-permute-start.1 = (bf16[2,3,32,768]{3,2,1,0:T(8,128)(2,1)S(1)}, bf16[2,3,32,768]{3,2,1,0:T(8,128)(2,1)S(1)}, u32[]{:S(2)}, u32[]{:S(2)}) collective-permute-start(bf16[2,3,32,768]{3,2,1,0:T(8,128)(2,1)S(1)} %cross_rows.1), channel_id=1, source_target_pairs={{0,63},{3,4},{4,3},{7,8},{8,7},{11,12},{12,11},{15,16},{16,15},{19... | collective-permute-start | bytes 884744 | tf_op jit(solution)/shard_map/ppermute | solution.py:299
  12.9 5.1 %collective-permute-start = (bf16[3,32,768]{2,1,0:T(8,128)(2,1)S(1)}, bf16[3,32,768]{2,1,0:T(8,128)(2,1)S(1)}, u32[]{:S(2)}, u32[]{:S(2)}) collective-permute-start(bf16[3,32,768]{2,1,0:T(8,128)(2,1)S(1)} %get-tuple-element.43.refs_1_), channel_id=1, source_target_pairs={{0,1},{1,0},{2,3},{3,2},{4,5},{5,4},{6,7},{7,6},{8,9},{9,8},{10,11... | collective-permute-start | bytes 442376 | tf_op jit(solution)/shard_map/ppermute | solution.py:313
  16.0 2.6 %collective-permute-start.4 = (bf16[3,32,768]{2,1,0:T(8,128)(2,1)S(1)}, bf16[3,32,768]{2,1,0:T(8,128)(2,1)S(1)}, u32[]{:S(2)}, u32[]{:S(2)}) collective-permute-start(bf16[3,32,768]{2,1,0:T(8,128)(2,1)S(1)} %get-tuple-element.53), channel_id=1, source_target_pairs={{0,64},{1,65},{2,66},{3,67},{4,68},{5,69},{6,70},{7,71},{8,72},{9,... | collective-permute-start | bytes 442376 | tf_op jit(solution)/shard_map/ppermute | solution.py:323
  16.7 4.2 %collective-permute-start.5 = (bf16[5,32,768]{2,1,0:T(8,128)(2,1)S(1)}, bf16[5,32,768]{2,1,0:T(8,128)(2,1)S(1)}, u32[]{:S(2)}, u32[]{:S(2)}) collective-permute-start(bf16[5,32,768]{2,1,0:T(8,128)(2,1)S(1)} %get-tuple-element.56), channel_id=1, source_target_pairs={{0,64},{1,65},{2,66},{3,67},{4,68},{5,69},{6,70},{7,71},{8,72},{9,... | collective-permute-start | bytes 737288 | tf_op jit(solution)/shard_map/ppermute | solution.py:325
  17.4 2.8 %collective-permute-start.7 = (bf16[3,32,768]{2,1,0:T(8,128)(2,1)S(1)}, bf16[3,32,768]{2,1,0:T(8,128)(2,1)S(1)}, u32[]{:S(2)}, u32[]{:S(2)}) collective-permute-start(bf16[3,32,768]{2,1,0:T(8,128)(2,1)S(1)} %get-tuple-element.57), channel_id=1, source_target_pairs={{0,127},{3,68},{4,67},{7,72},{8,71},{11,76},{12,75},{15,80},{16,79... | collective-permute-start | bytes 442376 | tf_op jit(solution)/shard_map/ppermute | solution.py:324
  18.8 2.8 %collective-permute-start.3 = (bf16[3,32,768]{2,1,0:T(8,128)(2,1)S(1)}, bf16[3,32,768]{2,1,0:T(8,128)(2,1)S(1)}, u32[]{:S(2)}, u32[]{:S(2)}) collective-permute-start(bf16[3,32,768]{2,1,0:T(8,128)(2,1)S(1)} %get-tuple-element.52), channel_id=1, source_target_pairs={{0,64},{1,65},{2,66},{3,67},{4,68},{5,69},{6,70},{7,71},{8,72},{9,... | collective-permute-start | bytes 442376 | tf_op jit(solution)/shard_map/ppermute | solution.py:323
  19.5 4.1 %collective-permute-start.10 = (bf16[3,32,768]{2,1,0:T(8,128)(2,1)S(1)}, bf16[3,32,768]{2,1,0:T(8,128)(2,1)S(1)}, u32[]{:S(2)}, u32[]{:S(2)}) collective-permute-start(bf16[3,32,768]{2,1,0:T(8,128)(2,1)S(1)} %get-tuple-element.61), channel_id=1, source_target_pairs={{0,127},{3,68},{4,67},{7,72},{8,71},{11,76},{12,75},{15,80},{16,79... | collective-permute-start | bytes 442376 | tf_op jit(solution)/shard_map/ppermute | solution.py:324
  20.2 4.1 %collective-permute-start.8 = (bf16[5,32,768]{2,1,0:T(8,128)(2,1)S(1)}, bf16[5,32,768]{2,1,0:T(8,128)(2,1)S(1)}, u32[]{:S(2)}, u32[]{:S(2)}) collective-permute-start(bf16[5,32,768]{2,1,0:T(8,128)(2,1)S(1)} %get-tuple-element.60), channel_id=1, source_target_pairs={{0,64},{1,65},{2,66},{3,67},{4,68},{5,69},{6,70},{7,71},{8,72},{9,... | collective-permute-start | bytes 737288 | tf_op jit(solution)/shard_map/ppermute | solution.py:325
  21.7 2.6 %collective-permute-start.9 = (bf16[3,32,768]{2,1,0:T(8,128)(2,1)S(1)}, bf16[3,32,768]{2,1,0:T(8,128)(2,1)S(1)}, u32[]{:S(2)}, u32[]{:S(2)}) collective-permute-start(bf16[3,32,768]{2,1,0:T(8,128)(2,1)S(1)} %collective-permute-done.3.refs_1_), channel_id=1, source_target_pairs={{0,1},{1,0},{2,3},{3,2},{4,5},{5,4},{6,7},{7,6},{8,9},{9,8},{10,11... | collective-permute-start | bytes 442376 | tf_op jit(solution)/shard_map/ppermute | solution.py:313
  22.3 2.7 %collective-permute-start.12 = (bf16[3,32,768]{2,1,0:T(8,128)(2,1)S(1)}, bf16[3,32,768]{2,1,0:T(8,128)(2,1)S(1)}, u32[]{:S(2)}, u32[]{:S(2)}) collective-permute-start(bf16[3,32,768]{2,1,0:T(8,128)(2,1)S(1)} %get-tuple-element.63), channel_id=1, source_target_pairs={{64,128},{65,129},{66,130},{67,131},{68,132},{69,133},{70,134},{71... | collective-permute-start | bytes 442376 | tf_op jit(solution)/shard_map/ppermute | solution.py:323
  22.9 4.2 %collective-permute-start.13 = (bf16[5,32,768]{2,1,0:T(8,128)(2,1)S(1)}, bf16[5,32,768]{2,1,0:T(8,128)(2,1)S(1)}, u32[]{:S(2)}, u32[]{:S(2)}) collective-permute-start(bf16[5,32,768]{2,1,0:T(8,128)(2,1)S(1)} %get-tuple-element.66), channel_id=1, source_target_pairs={{64,128},{65,129},{66,130},{67,131},{68,132},{69,133},{70,134},{71... | collective-permute-start | bytes 737288 | tf_op jit(solution)/shard_map/ppermute | solution.py:325
  23.6 2.8 %collective-permute-start.15 = (bf16[3,32,768]{2,1,0:T(8,128)(2,1)S(1)}, bf16[3,32,768]{2,1,0:T(8,128)(2,1)S(1)}, u32[]{:S(2)}, u32[]{:S(2)}) collective-permute-start(bf16[3,32,768]{2,1,0:T(8,128)(2,1)S(1)} %get-tuple-element.67), channel_id=1, source_target_pairs={{64,191},{67,132},{68,131},{71,136},{72,135},{75,140},{76,139},{79... | collective-permute-start | bytes 442376 | tf_op jit(solution)/shard_map/ppermute | solution.py:324
  25.1 2.7 %collective-permute-start.11 = (bf16[3,32,768]{2,1,0:T(8,128)(2,1)S(1)}, bf16[3,32,768]{2,1,0:T(8,128)(2,1)S(1)}, u32[]{:S(2)}, u32[]{:S(2)}) collective-permute-start(bf16[3,32,768]{2,1,0:T(8,128)(2,1)S(1)} %get-tuple-element.62), channel_id=1, source_target_pairs={{64,128},{65,129},{66,130},{67,131},{68,132},{69,133},{70,134},{71... | collective-permute-start | bytes 442376 | tf_op jit(solution)/shard_map/ppermute | solution.py:323
  25.8 5.4 %collective-permute-start.18 = (bf16[3,32,768]{2,1,0:T(8,128)(2,1)S(1)}, bf16[3,32,768]{2,1,0:T(8,128)(2,1)S(1)}, u32[]{:S(2)}, u32[]{:S(2)}) collective-permute-start(bf16[3,32,768]{2,1,0:T(8,128)(2,1)S(1)} %get-tuple-element.71), channel_id=1, source_target_pairs={{64,191},{67,132},{68,131},{71,136},{72,135},{75,140},{76,139},{79... | collective-permute-start | bytes 442376 | tf_op jit(solution)/shard_map/ppermute | solution.py:324
  26.5 6.0 %collective-permute-start.16 = (bf16[5,32,768]{2,1,0:T(8,128)(2,1)S(1)}, bf16[5,32,768]{2,1,0:T(8,128)(2,1)S(1)}, u32[]{:S(2)}, u32[]{:S(2)}) collective-permute-start(bf16[5,32,768]{2,1,0:T(8,128)(2,1)S(1)} %get-tuple-element.70), channel_id=1, source_target_pairs={{64,128},{65,129},{66,130},{67,131},{68,132},{69,133},{70,134},{71... | collective-permute-start | bytes 737288 | tf_op jit(solution)/shard_map/ppermute | solution.py:325
  27.8 4.7 %collective-permute-start.17 = (bf16[3,32,768]{2,1,0:T(8,128)(2,1)S(1)}, bf16[3,32,768]{2,1,0:T(8,128)(2,1)S(1)}, u32[]{:S(2)}, u32[]{:S(2)}) collective-permute-start(bf16[3,32,768]{2,1,0:T(8,128)(2,1)S(1)} %collective-permute-done.11.refs_1_), channel_id=1, source_target_pairs={{0,1},{1,0},{2,3},{3,2},{4,5},{5,4},{6,7},{7,6},{8,9},{9,8},{10,11... | collective-permute-start | bytes 442376 | tf_op jit(solution)/shard_map/ppermute | solution.py:313
  28.6 41.3 %collective-permute-start.20 = (bf16[3,32,768]{2,1,0:T(8,128)(2,1)S(1)}, bf16[3,32,768]{2,1,0:T(8,128)(2,1)S(1)}, u32[]{:S(2)}, u32[]{:S(2)}) collective-permute-start(bf16[3,32,768]{2,1,0:T(8,128)(2,1)S(1)} %get-tuple-element.73), channel_id=1, source_target_pairs={{128,192},{129,193},{130,194},{131,195},{132,196},{133,197},{134,1... | collective-permute-start | bytes 442376 | tf_op jit(solution)/shard_map/ppermute | solution.py:323
  29.9 46.6 %collective-permute-start.21 = (bf16[5,32,768]{2,1,0:T(8,128)(2,1)S(1)}, bf16[5,32,768]{2,1,0:T(8,128)(2,1)S(1)}, u32[]{:S(2)}, u32[]{:S(2)}) collective-permute-start(bf16[5,32,768]{2,1,0:T(8,128)(2,1)S(1)} %get-tuple-element.76), channel_id=1, source_target_pairs={{128,192},{129,193},{130,194},{131,195},{132,196},{133,197},{134,1... | collective-permute-start | bytes 737288 | tf_op jit(solution)/shard_map/ppermute | solution.py:325
  31.2 43.9 %collective-permute-start.23 = (bf16[3,32,768]{2,1,0:T(8,128)(2,1)S(1)}, bf16[3,32,768]{2,1,0:T(8,128)(2,1)S(1)}, u32[]{:S(2)}, u32[]{:S(2)}) collective-permute-start(bf16[3,32,768]{2,1,0:T(8,128)(2,1)S(1)} %get-tuple-element.77), channel_id=1, source_target_pairs={{128,255},{131,196},{132,195},{135,200},{136,199},{139,204},{140,2... | collective-permute-start | bytes 442376 | tf_op jit(solution)/shard_map/ppermute | solution.py:324
  69.8 6.6 %collective-permute-start.22 = (bf16[3,32,768]{2,1,0:T(8,128)(2,1)S(1)}, bf16[3,32,768]{2,1,0:T(8,128)(2,1)S(1)}, u32[]{:S(2)}, u32[]{:S(2)}) collective-permute-start(bf16[3,32,768]{2,1,0:T(8,128)(2,1)S(1)} %collective-permute-done.20.refs_1_), channel_id=1, source_target_pairs={{0,1},{1,0},{2,3},{3,2},{4,5},{5,4},{6,7},{7,6},{8,9},{9,8},{10,11... | collective-permute-start | bytes 442376 | tf_op jit(solution)/shard_map/ppermute | solution.py:313
  69.9 13.6 %collective-permute-start.19 = (bf16[3,32,768]{2,1,0:T(8,128)(2,1)S(1)}, bf16[3,32,768]{2,1,0:T(8,128)(2,1)S(1)}, u32[]{:S(2)}, u32[]{:S(2)}) collective-permute-start(bf16[3,32,768]{2,1,0:T(8,128)(2,1)S(1)} %get-tuple-element.72), channel_id=1, source_target_pairs={{128,192},{129,193},{130,194},{131,195},{132,196},{133,197},{134,1... | collective-permute-start | bytes 442376 | tf_op jit(solution)/shard_map/ppermute | solution.py:323
  71.2 15.6 %collective-permute-start.26 = (bf16[3,32,768]{2,1,0:T(8,128)(2,1)S(1)}, bf16[3,32,768]{2,1,0:T(8,128)(2,1)S(1)}, u32[]{:S(2)}, u32[]{:S(2)}) collective-permute-start(bf16[3,32,768]{2,1,0:T(8,128)(2,1)S(1)} %get-tuple-element.80), channel_id=1, source_target_pairs={{128,255},{131,196},{132,195},{135,200},{136,199},{139,204},{140,2... | collective-permute-start | bytes 442376 | tf_op jit(solution)/shard_map/ppermute | solution.py:324
  75.1 14.7 %collective-permute-start.24 = (bf16[5,32,768]{2,1,0:T(8,128)(2,1)S(1)}, bf16[5,32,768]{2,1,0:T(8,128)(2,1)S(1)}, u32[]{:S(2)}, u32[]{:S(2)}) collective-permute-start(bf16[5,32,768]{2,1,0:T(8,128)(2,1)S(1)} %get-tuple-element.79), channel_id=1, source_target_pairs={{128,192},{129,193},{130,194},{131,195},{132,196},{133,197},{134,1... | collective-permute-start | bytes 737288 | tf_op jit(solution)/shard_map/ppermute | solution.py:325
  83.5 6.3 %collective-permute-start.25 = (bf16[3,32,768]{2,1,0:T(8,128)(2,1)S(1)}, bf16[3,32,768]{2,1,0:T(8,128)(2,1)S(1)}, u32[]{:S(2)}, u32[]{:S(2)}) collective-permute-start(bf16[3,32,768]{2,1,0:T(8,128)(2,1)S(1)} %collective-permute-done.19.refs_1_), channel_id=1, source_target_pairs={{0,1},{1,0},{2,3},{3,2},{4,5},{5,4},{6,7},{7,6},{8,9},{9,8},{10,11... | collective-permute-start | bytes 442376 | tf_op jit(solution)/shard_map/ppermute | solution.py:313
  (3 other events, 6.7 us)

commit v5 on v4

--- a/solution.py
+++ b/solution.py
@@ -144,7 +144,6 @@
         get_out.start()
         if last:
             keep_earlier = pltpu.make_async_copy(earlier, stash.at[0, micro - 1], sems.at[2])
-            keep_earlier.start()
         @pl.loop(0, channels // LANES)
         def _(group):
             lanes = pl.ds(pl.multiple_of(group * LANES, LANES), LANES)
@@ -169,6 +168,8 @@
             normal[pl.ds(pl.multiple_of(row * width, width), width), :] = normed
 
         get_in.wait()
+        if last:
+            keep_earlier.start()
         for start in range(0, hidden, chunk):
             part = slice(start, start + chunk)
             inner = jnp.dot(normal[...], w_in[:, part], preferred_element_type=F32) + inner_bias[:, part]

time: 98.5 us -> 98.2 us (level)
  no operation moved by 1% of the time
where the time goes in v5:
time: 98.2 us; the launch traced here: 97.6 us
  waiting for transfers between devices  45.8 us (47%)
  starting transfers between devices  27.4 us (28%)
  Pallas kernels  23.5 us (24%)
    ppermute x6, waiting for transfers between devices, body(): near = lax.ppermute(relayed[0], axes, relay_pairs(section, same))  36.8 us
    pallas_call x8, Pallas kernels, run_block(): pl.pallas_call(functools.partial(block_kernel, micro, last, final, 768),...  18.5 us
    ppermute x1, starting transfers between devices, body(): cross = lax.ppermute(cross, axes, near_pairs)  9.4 us
    ppermute x6, waiting for transfers between devices, body(): cross = lax.ppermute(relayed[2], axes, relay_pairs(section, facing))  5.61 us
    ppermute x6, starting transfers between devices, body(): far = lax.ppermute(relayed[1], axes, relay_pairs(section, same))  5.28 us
    ppermute x6, starting transfers between devices, body(): cross = lax.ppermute(relayed[2], axes, relay_pairs(section, facing))  5.26 us
    ppermute x6, starting transfers between devices, body(): near = lax.ppermute(relayed[0], axes, relay_pairs(section, same))  5.21 us
    pallas_call x2, Pallas kernels, mirrored_rows(): pl.pallas_call(kernel, out_shape=[pltpu.VMEM(shape, BF) for shape in shap...  3.32 us
  transfers between devices with their start and end apart: 27, of which 6 were waited for; matrix products, arithmetic and copies ran while one was open for 0% of the time, Pallas kernels for 14%

profile of v5, /device:TPU:24, one launch (start us, length us, event | category | flops | bytes accessed | tf_op | source)
XLA Modules:
  0.0 97.6 jit_solution(4207705522543477696)
XLA Ops:
  0.1 1.5 %cross_rows.1 = bf16[2,3,32,768]{3,2,1,0:T(8,128)(2,1)S(1)} custom-call(s32[2]{0:T(128)S(1)} %pad_add_fusion.3.flags.refs_0_, bf16[2,8,32,768]{3,2,1,0:T(8,128)(2,1)} %images.3), custom_call_target="tpu_custom_call" | custom-call | bytes 2097152 | tf_op jit(solution)/shard_map/cross_rows/pallas_call | solution.py:58
  1.6 9.4 %collective-permute-start.1 = (bf16[2,3,32,768]{3,2,1,0:T(8,128)(2,1)S(1)}, bf16[2,3,32,768]{3,2,1,0:T(8,128)(2,1)S(1)}, u32[]{:S(2)}, u32[]{:S(2)}) collective-permute-start(bf16[2,3,32,768]{3,2,1,0:T(8,128)(2,1)S(1)} %cross_rows.1), channel_id=1, source_target_pairs={{0,63},{3,4},{4,3},{7,8},{8,7},{11,12},{12,11},{15,16},{16,15},{19... | collective-permute-start | bytes 884744 | tf_op jit(solution)/shard_map/ppermute | solution.py:300
  11.0 1.8 %own_rows.1 = (bf16[3,32,768]{2,1,0:T(8,128)(2,1)S(1)}, bf16[3,32,768]{2,1,0:T(8,128)(2,1)S(1)}, bf16[5,32,768]{2,1,0:T(8,128)(2,1)S(1)}, bf16[5,32,768]{2,1,0:T(8,128)(2,1)S(1)}) custom-call(s32[2]{0:T(128)S(1)} %pad_add_fusion.3.flags.refs_0_, bf16[2,8,32,768]{3,2,1,0:T(8,128)(2,1)} %images.3), custom_call_target="tpu_custom_call" | custom-call | bytes 2097152 | tf_op jit(solution)/shard_map/own_rows/pallas_call | solution.py:58
  13.4 1.6 %setup.1 = (bf16[49,16,768]{2,1,0:T(8,128)(2,1)S(1)}, f32[5,1,768]{2,1,0:T(1,128)S(1)}, f32[1,3072]{1,0:T(1,128)S(1)}, bf16[32,224]{1,0:T(8,128)(2,1)S(1)}) custom-call(s32[2]{0:T(128)S(1)} %pad_add_fusion.3.flags.refs_0_, bf16[1,7,7,768]{3,2,1,0:T(8,128)(2,1)} %weight.1, f32[1,768]{1,0:T(1,128)} %conv_bias.1, f32[1,768]{1,0:T(1,128)} %gain.1, ...), custom_call_target="tpu_custom_call" | custom-call | bytes 4194304 | tf_op jit(solution)/shard_map/setup/pallas_call | solution.py:94
  16.0 0.7 collective-permute-start.4
  16.7 0.7 collective-permute-start.5
  17.4 0.7 collective-permute-start.7
  20.2 0.7 collective-permute-start.8
  20.9 0.8 block.10
  22.9 0.7 collective-permute-start.13
  26.5 0.7 collective-permute-start.16
  27.8 0.8 collective-permute-start.17
  28.6 1.3 %collective-permute-start.20 = (bf16[3,32,768]{2,1,0:T(8,128)(2,1)S(1)}, bf16[3,32,768]{2,1,0:T(8,128)(2,1)S(1)}, u32[]{:S(2)}, u32[]{:S(2)}) collective-permute-start(bf16[3,32,768]{2,1,0:T(8,128)(2,1)S(1)} %get-tuple-element.73), channel_id=1, source_target_pairs={{128,192},{129,193},{130,194},{131,195},{132,196},{133,197},{134,1... | collective-permute-start | bytes 442376 | tf_op jit(solution)/shard_map/ppermute | solution.py:324
  29.9 1.3 %collective-permute-start.21 = (bf16[5,32,768]{2,1,0:T(8,128)(2,1)S(1)}, bf16[5,32,768]{2,1,0:T(8,128)(2,1)S(1)}, u32[]{:S(2)}, u32[]{:S(2)}) collective-permute-start(bf16[5,32,768]{2,1,0:T(8,128)(2,1)S(1)} %get-tuple-element.76), channel_id=1, source_target_pairs={{128,192},{129,193},{130,194},{131,195},{132,196},{133,197},{134,1... | collective-permute-start | bytes 737288 | tf_op jit(solution)/shard_map/ppermute | solution.py:326
  31.2 1.3 %collective-permute-start.23 = (bf16[3,32,768]{2,1,0:T(8,128)(2,1)S(1)}, bf16[3,32,768]{2,1,0:T(8,128)(2,1)S(1)}, u32[]{:S(2)}, u32[]{:S(2)}) collective-permute-start(bf16[3,32,768]{2,1,0:T(8,128)(2,1)S(1)} %get-tuple-element.77), channel_id=1, source_target_pairs={{128,255},{131,196},{132,195},{135,200},{136,199},{139,204},{140,2... | collective-permute-start | bytes 442376 | tf_op jit(solution)/shard_map/ppermute | solution.py:325
  33.1 36.7 %collective-permute-done.20.refs_1_ = bf16[3,32,768]{2,1,0:T(8,128)(2,1)S(1)} collective-permute-done((bf16[3,32,768]{2,1,0:T(8,128)(2,1)S(1)}, bf16[3,32,768]{2,1,0:T(8,128)(2,1)S(1)}, u32[]{:S(2)}, u32[]{:S(2)}) %collective-permute-start.20) | collective-permute-done | bytes 147488 | tf_op jit(solution)/shard_map/ppermute | solution.py:324
  69.9 1.3 %collective-permute-start.19 = (bf16[3,32,768]{2,1,0:T(8,128)(2,1)S(1)}, bf16[3,32,768]{2,1,0:T(8,128)(2,1)S(1)}, u32[]{:S(2)}, u32[]{:S(2)}) collective-permute-start(bf16[3,32,768]{2,1,0:T(8,128)(2,1)S(1)} %get-tuple-element.72), channel_id=1, source_target_pairs={{128,192},{129,193},{130,194},{131,195},{132,196},{133,197},{134,1... | collective-permute-start | bytes 442376 | tf_op jit(solution)/shard_map/ppermute | solution.py:324
  71.2 1.3 %collective-permute-start.26 = (bf16[3,32,768]{2,1,0:T(8,128)(2,1)S(1)}, bf16[3,32,768]{2,1,0:T(8,128)(2,1)S(1)}, u32[]{:S(2)}, u32[]{:S(2)}) collective-permute-start(bf16[3,32,768]{2,1,0:T(8,128)(2,1)S(1)} %get-tuple-element.80), channel_id=1, source_target_pairs={{128,255},{131,196},{132,195},{135,200},{136,199},{139,204},{140,2... | collective-permute-start | bytes 442376 | tf_op jit(solution)/shard_map/ppermute | solution.py:325
  72.5 2.5 %collective-permute-done.23.refs_4_ = bf16[3,32,768]{2,1,0:T(8,128)(2,1)S(1)} collective-permute-done((bf16[3,32,768]{2,1,0:T(8,128)(2,1)S(1)}, bf16[3,32,768]{2,1,0:T(8,128)(2,1)S(1)}, u32[]{:S(2)}, u32[]{:S(2)}) %collective-permute-start.23) | collective-permute-done | bytes 147488 | tf_op jit(solution)/shard_map/ppermute | solution.py:325
  75.1 1.3 %collective-permute-start.24 = (bf16[5,32,768]{2,1,0:T(8,128)(2,1)S(1)}, bf16[5,32,768]{2,1,0:T(8,128)(2,1)S(1)}, u32[]{:S(2)}, u32[]{:S(2)}) collective-permute-start(bf16[5,32,768]{2,1,0:T(8,128)(2,1)S(1)} %get-tuple-element.79), channel_id=1, source_target_pairs={{128,192},{129,193},{130,194},{131,195},{132,196},{133,197},{134,1... | collective-permute-start | bytes 737288 | tf_op jit(solution)/shard_map/ppermute | solution.py:326
  76.5 7.0 %block.14.refs_11_ = bf16[8,32,768]{2,1,0:T(8,128)(2,1)S(1)} custom-call(s32[2]{0:T(128)S(1)} %pad_add_fusion.refs_0_, bf16[3,32,768]{2,1,0:T(8,128)(2,1)S(1)} %collective-permute-done.20.refs_1_, bf16[5,32,768]{2,1,0:T(8,128)(2,1)S(1)} %collective-permute-done.21.refs_2_, bf16[3,32,768]{2,1,0:T(8,128)(2,1)S(1)} %collective-permute-done.22.refs_3_, ...), custom_call_target="tpu_custom_call" | custom-call | flops 8589934592 | bytes 1024 | tf_op jit(solution)/shard_map/block/pallas_call | solution.py:256
  83.6 3.1 %collective-permute-done.26.refs_4_ = bf16[3,32,768]{2,1,0:T(8,128)(2,1)S(1)} collective-permute-done((bf16[3,32,768]{2,1,0:T(8,128)(2,1)S(1)}, bf16[3,32,768]{2,1,0:T(8,128)(2,1)S(1)}, u32[]{:S(2)}, u32[]{:S(2)}) %collective-permute-start.26) | collective-permute-done | bytes 147488 | tf_op jit(solution)/shard_map/ppermute | solution.py:325
  86.6 2.9 %collective-permute-done.24.refs_2_ = bf16[5,32,768]{2,1,0:T(8,128)(2,1)S(1)} collective-permute-done((bf16[5,32,768]{2,1,0:T(8,128)(2,1)S(1)}, bf16[5,32,768]{2,1,0:T(8,128)(2,1)S(1)}, u32[]{:S(2)}, u32[]{:S(2)}) %collective-permute-start.24) | collective-permute-done | bytes 245792 | tf_op jit(solution)/shard_map/ppermute | solution.py:326
  89.5 7.8 %block.15 = bf16[1,2,8,32,768]{4,3,2,1,0:T(8,128)(2,1)} custom-call(s32[2]{0:T(128)S(1)} %pad_add_fusion.refs_0_, bf16[3,32,768]{2,1,0:T(8,128)(2,1)S(1)} %collective-permute-done.19.refs_1_, bf16[5,32,768]{2,1,0:T(8,128)(2,1)S(1)} %collective-permute-done.24.refs_2_, ...), custom_call_target="tpu_custom_call", output_to_operand_aliasing={{}: (12, {})} | custom-call | flops 1048576 | bytes 1024 | tf_op jit(solution)/shard_map/block/pallas_call | solution.py:256
  (45 shorter events, 9.3 us)
Async XLA Ops:
  1.6 13.8 %collective-permute-start.1 = (bf16[2,3,32,768]{3,2,1,0:T(8,128)(2,1)S(1)}, bf16[2,3,32,768]{3,2,1,0:T(8,128)(2,1)S(1)}, u32[]{:S(2)}, u32[]{:S(2)}) collective-permute-start(bf16[2,3,32,768]{3,2,1,0:T(8,128)(2,1)S(1)} %cross_rows.1), channel_id=1, source_target_pairs={{0,63},{3,4},{4,3},{7,8},{8,7},{11,12},{12,11},{15,16},{16,15},{19... | collective-permute-start | bytes 884744 | tf_op jit(solution)/shard_map/ppermute | solution.py:300
  12.9 5.1 %collective-permute-start = (bf16[3,32,768]{2,1,0:T(8,128)(2,1)S(1)}, bf16[3,32,768]{2,1,0:T(8,128)(2,1)S(1)}, u32[]{:S(2)}, u32[]{:S(2)}) collective-permute-start(bf16[3,32,768]{2,1,0:T(8,128)(2,1)S(1)} %get-tuple-element.43.refs_1_), channel_id=1, source_target_pairs={{0,1},{1,0},{2,3},{3,2},{4,5},{5,4},{6,7},{7,6},{8,9},{9,8},{10,11... | collective-permute-start | bytes 442376 | tf_op jit(solution)/shard_map/ppermute | solution.py:314
  16.0 2.6 %collective-permute-start.4 = (bf16[3,32,768]{2,1,0:T(8,128)(2,1)S(1)}, bf16[3,32,768]{2,1,0:T(8,128)(2,1)S(1)}, u32[]{:S(2)}, u32[]{:S(2)}) collective-permute-start(bf16[3,32,768]{2,1,0:T(8,128)(2,1)S(1)} %get-tuple-element.53), channel_id=1, source_target_pairs={{0,64},{1,65},{2,66},{3,67},{4,68},{5,69},{6,70},{7,71},{8,72},{9,... | collective-permute-start | bytes 442376 | tf_op jit(solution)/shard_map/ppermute | solution.py:324
  16.7 4.2 %collective-permute-start.5 = (bf16[5,32,768]{2,1,0:T(8,128)(2,1)S(1)}, bf16[5,32,768]{2,1,0:T(8,128)(2,1)S(1)}, u32[]{:S(2)}, u32[]{:S(2)}) collective-permute-start(bf16[5,32,768]{2,1,0:T(8,128)(2,1)S(1)} %get-tuple-element.56), channel_id=1, source_target_pairs={{0,64},{1,65},{2,66},{3,67},{4,68},{5,69},{6,70},{7,71},{8,72},{9,... | collective-permute-start | bytes 737288 | tf_op jit(solution)/shard_map/ppermute | solution.py:326
  17.4 2.8 %collective-permute-start.7 = (bf16[3,32,768]{2,1,0:T(8,128)(2,1)S(1)}, bf16[3,32,768]{2,1,0:T(8,128)(2,1)S(1)}, u32[]{:S(2)}, u32[]{:S(2)}) collective-permute-start(bf16[3,32,768]{2,1,0:T(8,128)(2,1)S(1)} %get-tuple-element.57), channel_id=1, source_target_pairs={{0,127},{3,68},{4,67},{7,72},{8,71},{11,76},{12,75},{15,80},{16,79... | collective-permute-start | bytes 442376 | tf_op jit(solution)/shard_map/ppermute | solution.py:325
  18.8 2.8 %collective-permute-start.3 = (bf16[3,32,768]{2,1,0:T(8,128)(2,1)S(1)}, bf16[3,32,768]{2,1,0:T(8,128)(2,1)S(1)}, u32[]{:S(2)}, u32[]{:S(2)}) collective-permute-start(bf16[3,32,768]{2,1,0:T(8,128)(2,1)S(1)} %get-tuple-element.52), channel_id=1, source_target_pairs={{0,64},{1,65},{2,66},{3,67},{4,68},{5,69},{6,70},{7,71},{8,72},{9,... | collective-permute-start | bytes 442376 | tf_op jit(solution)/shard_map/ppermute | solution.py:324
  19.5 4.1 %collective-permute-start.10 = (bf16[3,32,768]{2,1,0:T(8,128)(2,1)S(1)}, bf16[3,32,768]{2,1,0:T(8,128)(2,1)S(1)}, u32[]{:S(2)}, u32[]{:S(2)}) collective-permute-start(bf16[3,32,768]{2,1,0:T(8,128)(2,1)S(1)} %get-tuple-element.61), channel_id=1, source_target_pairs={{0,127},{3,68},{4,67},{7,72},{8,71},{11,76},{12,75},{15,80},{16,79... | collective-permute-start | bytes 442376 | tf_op jit(solution)/shard_map/ppermute | solution.py:325
  20.2 4.1 %collective-permute-start.8 = (bf16[5,32,768]{2,1,0:T(8,128)(2,1)S(1)}, bf16[5,32,768]{2,1,0:T(8,128)(2,1)S(1)}, u32[]{:S(2)}, u32[]{:S(2)}) collective-permute-start(bf16[5,32,768]{2,1,0:T(8,128)(2,1)S(1)} %get-tuple-element.60), channel_id=1, source_target_pairs={{0,64},{1,65},{2,66},{3,67},{4,68},{5,69},{6,70},{7,71},{8,72},{9,... | collective-permute-start | bytes 737288 | tf_op jit(solution)/shard_map/ppermute | solution.py:326
  21.7 2.6 %collective-permute-start.9 = (bf16[3,32,768]{2,1,0:T(8,128)(2,1)S(1)}, bf16[3,32,768]{2,1,0:T(8,128)(2,1)S(1)}, u32[]{:S(2)}, u32[]{:S(2)}) collective-permute-start(bf16[3,32,768]{2,1,0:T(8,128)(2,1)S(1)} %collective-permute-done.3.refs_1_), channel_id=1, source_target_pairs={{0,1},{1,0},{2,3},{3,2},{4,5},{5,4},{6,7},{7,6},{8,9},{9,8},{10,11... | collective-permute-start | bytes 442376 | tf_op jit(solution)/shard_map/ppermute | solution.py:314
  22.3 2.7 %collective-permute-start.12 = (bf16[3,32,768]{2,1,0:T(8,128)(2,1)S(1)}, bf16[3,32,768]{2,1,0:T(8,128)(2,1)S(1)}, u32[]{:S(2)}, u32[]{:S(2)}) collective-permute-start(bf16[3,32,768]{2,1,0:T(8,128)(2,1)S(1)} %get-tuple-element.63), channel_id=1, source_target_pairs={{64,128},{65,129},{66,130},{67,131},{68,132},{69,133},{70,134},{71... | collective-permute-start | bytes 442376 | tf_op jit(solution)/shard_map/ppermute | solution.py:324
  22.9 4.2 %collective-permute-start.13 = (bf16[5,32,768]{2,1,0:T(8,128)(2,1)S(1)}, bf16[5,32,768]{2,1,0:T(8,128)(2,1)S(1)}, u32[]{:S(2)}, u32[]{:S(2)}) collective-permute-start(bf16[5,32,768]{2,1,0:T(8,128)(2,1)S(1)} %get-tuple-element.66), channel_id=1, source_target_pairs={{64,128},{65,129},{66,130},{67,131},{68,132},{69,133},{70,134},{71... | collective-permute-start | bytes 737288 | tf_op jit(solution)/shard_map/ppermute | solution.py:326
  23.6 2.8 %collective-permute-start.15 = (bf16[3,32,768]{2,1,0:T(8,128)(2,1)S(1)}, bf16[3,32,768]{2,1,0:T(8,128)(2,1)S(1)}, u32[]{:S(2)}, u32[]{:S(2)}) collective-permute-start(bf16[3,32,768]{2,1,0:T(8,128)(2,1)S(1)} %get-tuple-element.67), channel_id=1, source_target_pairs={{64,191},{67,132},{68,131},{71,136},{72,135},{75,140},{76,139},{79... | collective-permute-start | bytes 442376 | tf_op jit(solution)/shard_map/ppermute | solution.py:325
  25.1 2.7 %collective-permute-start.11 = (bf16[3,32,768]{2,1,0:T(8,128)(2,1)S(1)}, bf16[3,32,768]{2,1,0:T(8,128)(2,1)S(1)}, u32[]{:S(2)}, u32[]{:S(2)}) collective-permute-start(bf16[3,32,768]{2,1,0:T(8,128)(2,1)S(1)} %get-tuple-element.62), channel_id=1, source_target_pairs={{64,128},{65,129},{66,130},{67,131},{68,132},{69,133},{70,134},{71... | collective-permute-start | bytes 442376 | tf_op jit(solution)/shard_map/ppermute | solution.py:324
  25.8 5.4 %collective-permute-start.18 = (bf16[3,32,768]{2,1,0:T(8,128)(2,1)S(1)}, bf16[3,32,768]{2,1,0:T(8,128)(2,1)S(1)}, u32[]{:S(2)}, u32[]{:S(2)}) collective-permute-start(bf16[3,32,768]{2,1,0:T(8,128)(2,1)S(1)} %get-tuple-element.71), channel_id=1, source_target_pairs={{64,191},{67,132},{68,131},{71,136},{72,135},{75,140},{76,139},{79... | collective-permute-start | bytes 442376 | tf_op jit(solution)/shard_map/ppermute | solution.py:325
  26.5 6.0 %collective-permute-start.16 = (bf16[5,32,768]{2,1,0:T(8,128)(2,1)S(1)}, bf16[5,32,768]{2,1,0:T(8,128)(2,1)S(1)}, u32[]{:S(2)}, u32[]{:S(2)}) collective-permute-start(bf16[5,32,768]{2,1,0:T(8,128)(2,1)S(1)} %get-tuple-element.70), channel_id=1, source_target_pairs={{64,128},{65,129},{66,130},{67,131},{68,132},{69,133},{70,134},{71... | collective-permute-start | bytes 737288 | tf_op jit(solution)/shard_map/ppermute | solution.py:326
  27.8 4.7 %collective-permute-start.17 = (bf16[3,32,768]{2,1,0:T(8,128)(2,1)S(1)}, bf16[3,32,768]{2,1,0:T(8,128)(2,1)S(1)}, u32[]{:S(2)}, u32[]{:S(2)}) collective-permute-start(bf16[3,32,768]{2,1,0:T(8,128)(2,1)S(1)} %collective-permute-done.11.refs_1_), channel_id=1, source_target_pairs={{0,1},{1,0},{2,3},{3,2},{4,5},{5,4},{6,7},{7,6},{8,9},{9,8},{10,11... | collective-permute-start | bytes 442376 | tf_op jit(solution)/shard_map/ppermute | solution.py:314
  28.6 41.3 %collective-permute-start.20 = (bf16[3,32,768]{2,1,0:T(8,128)(2,1)S(1)}, bf16[3,32,768]{2,1,0:T(8,128)(2,1)S(1)}, u32[]{:S(2)}, u32[]{:S(2)}) collective-permute-start(bf16[3,32,768]{2,1,0:T(8,128)(2,1)S(1)} %get-tuple-element.73), channel_id=1, source_target_pairs={{128,192},{129,193},{130,194},{131,195},{132,196},{133,197},{134,1... | collective-permute-start | bytes 442376 | tf_op jit(solution)/shard_map/ppermute | solution.py:324
  29.9 46.6 %collective-permute-start.21 = (bf16[5,32,768]{2,1,0:T(8,128)(2,1)S(1)}, bf16[5,32,768]{2,1,0:T(8,128)(2,1)S(1)}, u32[]{:S(2)}, u32[]{:S(2)}) collective-permute-start(bf16[5,32,768]{2,1,0:T(8,128)(2,1)S(1)} %get-tuple-element.76), channel_id=1, source_target_pairs={{128,192},{129,193},{130,194},{131,195},{132,196},{133,197},{134,1... | collective-permute-start | bytes 737288 | tf_op jit(solution)/shard_map/ppermute | solution.py:326
  31.2 43.9 %collective-permute-start.23 = (bf16[3,32,768]{2,1,0:T(8,128)(2,1)S(1)}, bf16[3,32,768]{2,1,0:T(8,128)(2,1)S(1)}, u32[]{:S(2)}, u32[]{:S(2)}) collective-permute-start(bf16[3,32,768]{2,1,0:T(8,128)(2,1)S(1)} %get-tuple-element.77), channel_id=1, source_target_pairs={{128,255},{131,196},{132,195},{135,200},{136,199},{139,204},{140,2... | collective-permute-start | bytes 442376 | tf_op jit(solution)/shard_map/ppermute | solution.py:325
  69.8 6.6 %collective-permute-start.22 = (bf16[3,32,768]{2,1,0:T(8,128)(2,1)S(1)}, bf16[3,32,768]{2,1,0:T(8,128)(2,1)S(1)}, u32[]{:S(2)}, u32[]{:S(2)}) collective-permute-start(bf16[3,32,768]{2,1,0:T(8,128)(2,1)S(1)} %collective-permute-done.20.refs_1_), channel_id=1, source_target_pairs={{0,1},{1,0},{2,3},{3,2},{4,5},{5,4},{6,7},{7,6},{8,9},{9,8},{10,11... | collective-permute-start | bytes 442376 | tf_op jit(solution)/shard_map/ppermute | solution.py:314
  69.9 13.6 %collective-permute-start.19 = (bf16[3,32,768]{2,1,0:T(8,128)(2,1)S(1)}, bf16[3,32,768]{2,1,0:T(8,128)(2,1)S(1)}, u32[]{:S(2)}, u32[]{:S(2)}) collective-permute-start(bf16[3,32,768]{2,1,0:T(8,128)(2,1)S(1)} %get-tuple-element.72), channel_id=1, source_target_pairs={{128,192},{129,193},{130,194},{131,195},{132,196},{133,197},{134,1... | collective-permute-start | bytes 442376 | tf_op jit(solution)/shard_map/ppermute | solution.py:324
  71.2 15.4 %collective-permute-start.26 = (bf16[3,32,768]{2,1,0:T(8,128)(2,1)S(1)}, bf16[3,32,768]{2,1,0:T(8,128)(2,1)S(1)}, u32[]{:S(2)}, u32[]{:S(2)}) collective-permute-start(bf16[3,32,768]{2,1,0:T(8,128)(2,1)S(1)} %get-tuple-element.80), channel_id=1, source_target_pairs={{128,255},{131,196},{132,195},{135,200},{136,199},{139,204},{140,2... | collective-permute-start | bytes 442376 | tf_op jit(solution)/shard_map/ppermute | solution.py:325
  75.1 14.5 %collective-permute-start.24 = (bf16[5,32,768]{2,1,0:T(8,128)(2,1)S(1)}, bf16[5,32,768]{2,1,0:T(8,128)(2,1)S(1)}, u32[]{:S(2)}, u32[]{:S(2)}) collective-permute-start(bf16[5,32,768]{2,1,0:T(8,128)(2,1)S(1)} %get-tuple-element.79), channel_id=1, source_target_pairs={{128,192},{129,193},{130,194},{131,195},{132,196},{133,197},{134,1... | collective-permute-start | bytes 737288 | tf_op jit(solution)/shard_map/ppermute | solution.py:326
  83.5 6.1 %collective-permute-start.25 = (bf16[3,32,768]{2,1,0:T(8,128)(2,1)S(1)}, bf16[3,32,768]{2,1,0:T(8,128)(2,1)S(1)}, u32[]{:S(2)}, u32[]{:S(2)}) collective-permute-start(bf16[3,32,768]{2,1,0:T(8,128)(2,1)S(1)} %collective-permute-done.19.refs_1_), channel_id=1, source_target_pairs={{0,1},{1,0},{2,3},{3,2},{4,5},{5,4},{6,7},{7,6},{8,9},{9,8},{10,11... | collective-permute-start | bytes 442376 | tf_op jit(solution)/shard_map/ppermute | solution.py:314
  (3 other events, 6.7 us)
